TPU v7x, 32 devices: a whole 2x2x4 slice. The times are simulated.
32 devices in a mesh: dp: 8 (over z, x), section: 4 (over y, core).
Axes of the slice: x: 2, y: 2, z: 4, core: 2. Of those that a mesh axis runs over, the one named last changes fastest.
Arguments:
- pieces: bfloat16 [2048, 7, 512], P(('dp', 'section')), may hold values from -6 to 6
- counts: int32 [2048], P(('dp', 'section')), may hold values from 1 to 7
- groups: int32 [2048], P(('dp', 'section')), may hold values from 0 to 7
- group_table: bfloat16 [8, 512], replicated, may hold values from -3 to 3
- attn_gain: bfloat16 [2, 512], replicated, may hold values from 0.5 to 1.5
- attn_qkv: bfloat16 [2, 512, 1536], replicated, may hold values from -0.25 to 0.25
- attn_out: bfloat16 [2, 512, 512], replicated, may hold values from -0.5 to 0.5
- attn_bias: bfloat16 [2, 512], replicated, may hold values from -2 to 2
- ffn_gain: bfloat16 [2, 512], replicated, may hold values from 0.5 to 1.5
- ffn_up: bfloat16 [2, 512, 2048], replicated, may hold values from -0.25 to 0.25
- ffn_up_bias: bfloat16 [2, 2048], replicated, may hold values from -3 to 3
- ffn_down: bfloat16 [2, 2048, 512], replicated, may hold values from -0.125 to 0.125
- ffn_down_bias: bfloat16 [2, 512], replicated, may hold values from -2 to 2
- final_gain: bfloat16 [512], replicated, may hold values from 0.5 to 1.5
- pool_weight: bfloat16 [512, 2048], replicated, may hold values from -0.25 to 0.25
- pool_bias: bfloat16 [2048], replicated, may hold values from -3 to 3
- emb_cotangent: bfloat16 [2048, 2048], P(('dp', 'section')), may hold values from -6 to 6
Outputs:
- embeddings: bfloat16 [2048, 2048], P(('dp', 'section'))
- input_grad: bfloat16 [2048, 7, 512], P(('dp', 'section'))
- table_grad: float32 [8, 512], P(None, 'dp')
- attn_gain_grad: float32 [2, 512], P(None, 'dp')
- attn_qkv_grad: float32 [2, 512, 1536], P(None, 'dp')
- attn_out_grad: float32 [2, 512, 512], P(None, 'dp')
- attn_bias_grad: float32 [2, 512], P(None, 'dp')
- ffn_gain_grad: float32 [2, 512], P(None, 'dp')
- ffn_up_grad: float32 [2, 512, 2048], P(None, 'dp')
- ffn_up_bias_grad: float32 [2, 2048], P(None, 'dp')
- ffn_down_grad: float32 [2, 2048, 512], P(None, 'dp')
- ffn_down_bias_grad: float32 [2, 512], P(None, 'dp')
- final_gain_grad: float32 [512], P('dp')
- pool_weight_grad: float32 [512, 2048], P('dp')
- pool_bias_grad: float32 [2048], P('dp')
All inputs are finite; a program needn't handle non-finite values.
Results may differ from a plain program's by a relative error of at most 0.015.
Values may be sent and summed in bfloat16 or wider, within the bound.
A program may use at most 192 MiB of HBM per device.

v0:
```python
import jax
import jax.numpy as jnp
from jax import lax
from jax.sharding import PartitionSpec as P

HEADS = 8


EPS = 1e-05
MASKED = -1e30
HIGH = lax.Precision.HIGHEST


def shortened(array):
    return jax.tree.map(lambda a: a.astype(jnp.bfloat16) if a.dtype == jnp.float32 else a, array)


def shifted_2(block, axis, distance):
    devices = range(lax.axis_size(axis))
    route = [(i - distance, i) for i in devices if i - distance in devices]
    return lax.ppermute(block, axis, route)


def from_root(array, axis, root):
    mine = lax.axis_index(axis) == root
    return lax.psum(jnp.where(mine, array, jnp.zeros_like(array)), axis)


def layer_norm(values, norm_gain):
    centre = values - jnp.mean(values, axis=-1, keepdims=True)
    spread = jnp.mean(centre * centre, axis=-1, keepdims=True)
    return centre * lax.rsqrt(spread + EPS) * norm_gain


def pool_mean(hidden, live_mask, norm_gain):
    entries, pieces = live_mask.shape
    normed = layer_norm(hidden, norm_gain).reshape(entries, pieces, -1)
    return jnp.sum(normed * live_mask[:, :, None], axis=1) / jnp.sum(
        live_mask, axis=1, keepdims=True
    )


def matmul_plain(left_side, right_side):
    return jnp.dot(left_side, right_side, preferred_element_type=jnp.float32)


def matmul_left(left_side, right_side):
    return lax.dot_general(
        left_side, right_side, (((0,), (0,)), ((), ())), preferred_element_type=jnp.float32
    )


def matmul_right(left_side, right_side):
    return lax.dot_general(
        left_side, right_side, (((1,), (1,)), ((), ())), preferred_element_type=jnp.float32
    )


def gelu_exact(values):
    return jax.nn.gelu(values, approximate=False)


def attend_forward(hidden, live_mask, weights):
    norm_gain, w_qkv, w_out, b_out = weights
    entries, pieces = live_mask.shape
    model_width = hidden.shape[1]
    head_size = model_width // HEADS
    normed, norm_back = jax.vjp(layer_norm, hidden, norm_gain)
    normed_low = normed.astype(jnp.bfloat16)
    projected = matmul_plain(normed_low, w_qkv).astype(jnp.bfloat16)
    projected = projected.reshape(entries, pieces, 3, HEADS, head_size)
    queries = projected[:, :, 0]
    key_rows = projected[:, :, 1]
    value_rows = projected[:, :, 2]
    scores = jnp.einsum(
        "eqhd,ekhd->ehqk", queries, key_rows, preferred_element_type=jnp.float32
    ) * head_size ** (-0.5)
    scores = jnp.where(live_mask[:, None, None, :] > 0.5, scores, MASKED)
    shifted = jnp.exp(scores - jnp.max(scores, axis=-1, keepdims=True))
    attention = shifted / jnp.sum(shifted, axis=-1, keepdims=True)
    attention_low = attention.astype(jnp.bfloat16)
    context = jnp.einsum(
        "ehqk,ekhd->eqhd", attention_low, value_rows, preferred_element_type=jnp.float32
    )
    context = context.astype(jnp.bfloat16).reshape(entries * pieces, model_width)
    section_out = (hidden + matmul_plain(context, w_out) + b_out).astype(jnp.bfloat16)
    saved_state = (
        norm_back,
        normed_low,
        queries,
        key_rows,
        value_rows,
        attention,
        attention_low,
        context,
    )
    return (section_out, saved_state)


def attend_backward(hidden, grad_low, live_mask, weights, grad_acc):
    norm_gain, w_qkv, w_out, b_out = weights
    entries, pieces = live_mask.shape
    model_width = hidden.shape[1]
    head_size = model_width // HEADS
    section_out, saved_state = attend_forward(hidden, live_mask, weights)
    norm_back, normed_low, queries, key_rows, value_rows, attention, attention_low, context = (
        saved_state
    )
    gain_sum, qkv_sum, out_sum, bias_sum = grad_acc
    grad_wide = grad_low.astype(jnp.float32)
    out_sum = out_sum + matmul_left(context, grad_low)
    bias_sum = bias_sum + jnp.sum(grad_wide, axis=0)
    d_context = (
        matmul_right(grad_low, w_out)
        .astype(jnp.bfloat16)
        .reshape(entries, pieces, HEADS, head_size)
    )
    d_attention = jnp.einsum(
        "eqhd,ekhd->ehqk", d_context, value_rows, preferred_element_type=jnp.float32
    )
    d_values = jnp.einsum(
        "ehqk,eqhd->ekhd", attention_low, d_context, preferred_element_type=jnp.float32
    )
    d_scores = attention * (d_attention - jnp.sum(attention * d_attention, axis=-1, keepdims=True))
    d_scores = d_scores.astype(jnp.bfloat16)
    d_queries = jnp.einsum(
        "ehqk,ekhd->eqhd", d_scores, key_rows, preferred_element_type=jnp.float32
    ) * head_size ** (-0.5)
    d_keys = jnp.einsum(
        "ehqk,eqhd->ekhd", d_scores, queries, preferred_element_type=jnp.float32
    ) * head_size ** (-0.5)
    d_projected = jnp.stack([d_queries, d_keys, d_values], axis=2).astype(jnp.bfloat16)
    d_projected = d_projected.reshape(entries * pieces, 3 * model_width)
    qkv_sum = qkv_sum + matmul_left(normed_low, d_projected)
    d_hidden, gain_term = norm_back(matmul_right(d_projected, w_qkv))
    return (d_hidden + grad_wide, (gain_sum + gain_term, qkv_sum, out_sum, bias_sum))


def feed_forward(hidden, weights):
    norm_gain, w_up, b_up, w_down, b_down = weights
    normed, norm_back = jax.vjp(layer_norm, hidden, norm_gain)
    normed_low = normed.astype(jnp.bfloat16)
    inner_act = matmul_plain(normed_low, w_up) + b_up
    activated, gelu_back = jax.vjp(gelu_exact, inner_act)
    activated_low = activated.astype(jnp.bfloat16)
    section_out = (hidden + matmul_plain(activated_low, w_down) + b_down).astype(jnp.bfloat16)
    return (section_out, (norm_back, normed_low, gelu_back, activated_low))


def feed_backward(grad_low, saved_state, weights, grad_acc):
    norm_gain, w_up, b_up, w_down, b_down = weights
    norm_back, normed_low, gelu_back, activated_low = saved_state
    gain_sum, up_sum, up_bias_sum, down_sum, down_bias_sum = grad_acc
    grad_wide = grad_low.astype(jnp.float32)
    down_sum = down_sum + matmul_left(activated_low, grad_low)
    down_bias_sum = down_bias_sum + jnp.sum(grad_wide, axis=0)
    d_inner = gelu_back(matmul_right(grad_low, w_down))[0].astype(jnp.bfloat16)
    up_sum = up_sum + matmul_left(normed_low, d_inner)
    up_bias_sum = up_bias_sum + jnp.sum(d_inner.astype(jnp.float32), axis=0)
    d_hidden, gain_term = norm_back(matmul_right(d_inner, w_up))
    return (
        d_hidden + grad_wide,
        (gain_sum + gain_term, up_sum, up_bias_sum, down_sum, down_bias_sum),
    )


def per_device(
    pieces,
    counts,
    groups,
    group_table,
    attn_gain,
    attn_qkv,
    attn_out,
    attn_bias,
    ffn_gain,
    ffn_up,
    ffn_up_bias,
    ffn_down,
    ffn_down_bias,
    final_gain,
    pool_weight,
    pool_bias,
    emb_cotangent,
):
    entries, pieces_max, model_width = pieces.shape
    token_rows = entries * pieces_max
    group_count = group_table.shape[0]
    layer_count = attn_qkv.shape[0]
    section_count = lax.axis_size("section")
    section_index = lax.axis_index("section")
    last_section = section_count - 1
    layer_index = section_index // 2
    half_kind = section_index % 2
    is_last = section_index == last_section
    entry_lists = lax.all_gather(jnp.stack([counts, groups]), "section", axis=1, tiled=True)
    all_counts = entry_lists[0].reshape(section_count, entries)
    all_groups = entry_lists[1].reshape(section_count, entries)
    all_pieces = lax.all_gather(pieces, "section", axis=0, tiled=True)
    all_pieces = all_pieces.reshape(section_count, entries, pieces_max, model_width)

    def layer_pick(array):
        return lax.dynamic_index_in_dim(array, layer_index, 0, keepdims=False)

    attn_weights = (
        layer_pick(attn_gain).astype(jnp.float32),
        layer_pick(attn_qkv),
        layer_pick(attn_out),
        layer_pick(attn_bias).astype(jnp.float32),
    )
    ffn_weights = (
        layer_pick(ffn_gain).astype(jnp.float32),
        layer_pick(ffn_up),
        layer_pick(ffn_up_bias).astype(jnp.float32),
        layer_pick(ffn_down),
        layer_pick(ffn_down_bias).astype(jnp.float32),
    )
    end_gain = final_gain.astype(jnp.float32)

    def micro_inputs(micro_slot):
        count_row = lax.dynamic_index_in_dim(all_counts, micro_slot, 0, keepdims=False)
        group_row = lax.dynamic_index_in_dim(all_groups, micro_slot, 0, keepdims=False)
        live_mask = lax.broadcasted_iota(jnp.int32, (entries, pieces_max), 1) < count_row[:, None]
        onehot = group_row[:, None] == lax.broadcasted_iota(jnp.int32, (entries, group_count), 1)
        return (live_mask.astype(jnp.float32), onehot.astype(jnp.float32))

    def forward_attend(hidden, live_mask):
        section_out, saved_state = attend_forward(hidden, live_mask, attn_weights)
        return (section_out, jnp.zeros((entries, model_width), jnp.bfloat16))

    def forward_feed(hidden, live_mask):
        section_out, saved_state = feed_forward(hidden, ffn_weights)
        pooled = pool_mean(section_out.astype(jnp.float32), live_mask, end_gain).astype(
            jnp.bfloat16
        )
        return (section_out, pooled)

    def forward_spare(hidden, live_mask):
        return (
            jnp.zeros((token_rows, model_width), jnp.bfloat16),
            jnp.zeros((entries, model_width), jnp.bfloat16),
        )

    ticks = 2 * section_count - 1
    received = jnp.zeros((token_rows, model_width), jnp.bfloat16)
    kept_inputs = jnp.zeros((section_count, token_rows, model_width), jnp.float32)
    pooled_all = jnp.zeros((section_count, entries, model_width), jnp.bfloat16)
    for tick_index in range(ticks):
        micro_batch = tick_index - section_index
        is_valid = (micro_batch >= 0) & (micro_batch < section_count)
        micro_slot = jnp.clip(micro_batch, 0, section_count - 1)
        live_mask, onehot = micro_inputs(micro_slot)
        piece_rows = lax.dynamic_index_in_dim(all_pieces, micro_slot, 0, keepdims=False)
        group_rows = matmul_plain(onehot.astype(jnp.bfloat16), group_table)
        hidden_in = jnp.where(
            section_index == 0,
            (piece_rows.astype(jnp.float32) + group_rows[:, None, :]).reshape(
                token_rows, model_width
            ),
            received.astype(jnp.float32),
        )
        branch_index = jnp.where(is_valid, half_kind, 2)
        section_out, pooled = lax.switch(
            branch_index, [forward_attend, forward_feed, forward_spare], hidden_in, live_mask
        )
        old_input = lax.dynamic_index_in_dim(kept_inputs, micro_slot, 0, keepdims=False)
        kept_inputs = lax.dynamic_update_index_in_dim(
            kept_inputs, jnp.where(is_valid, hidden_in, old_input), micro_slot, 0
        )
        old_pooled = lax.dynamic_index_in_dim(pooled_all, micro_slot, 0, keepdims=False)
        new_pooled = jnp.where(is_valid & is_last, pooled, old_pooled)
        pooled_all = lax.dynamic_update_index_in_dim(pooled_all, new_pooled, micro_slot, 0)
        if tick_index < ticks - 1:
            received = jax.tree.map(
                lambda part, own: part.astype(own.dtype),
                shifted_2(shortened(section_out), "section", 1),
                section_out,
            )
    pooled_shared = from_root(pooled_all, "section", last_section)
    own_pooled = lax.dynamic_index_in_dim(pooled_shared, section_index, 0, keepdims=False)
    embeddings = (matmul_plain(own_pooled, pool_weight) + pool_bias.astype(jnp.float32)).astype(
        jnp.bfloat16
    )
    pool_term = matmul_left(own_pooled, emb_cotangent)
    pool_bias_term = jnp.sum(emb_cotangent.astype(jnp.float32), axis=0)
    own_pool_grad = matmul_right(emb_cotangent, pool_weight).astype(jnp.bfloat16)
    pool_grads = lax.all_gather(own_pool_grad, "section", axis=0, tiled=True).reshape(
        section_count, entries, model_width
    )

    def backward_attend(hidden, grad_in, pool_grad, live_mask, grad_acc):
        d_hidden, attn_acc = attend_backward(hidden, grad_in, live_mask, attn_weights, grad_acc[0])
        return (d_hidden, (attn_acc, grad_acc[1], grad_acc[2]))

    def backward_feed(hidden, grad_in, pool_grad, live_mask, grad_acc):
        section_out, saved_state = feed_forward(hidden, ffn_weights)
        pooled, pool_back = jax.vjp(
            lambda values, norm_gain: pool_mean(values, live_mask, norm_gain),
            section_out.astype(jnp.float32),
            end_gain,
        )
        d_from_pool, d_end_gain = pool_back(pool_grad.astype(jnp.float32))
        grad_low = jnp.where(is_last, d_from_pool.astype(jnp.bfloat16), grad_in)
        end_sum = grad_acc[2] + jnp.where(is_last, d_end_gain, 0.0)
        d_hidden, ffn_acc = feed_backward(grad_low, saved_state, ffn_weights, grad_acc[1])
        return (d_hidden, (grad_acc[0], ffn_acc, end_sum))

    def backward_spare(hidden, grad_in, pool_grad, live_mask, grad_acc):
        return (jnp.zeros((token_rows, model_width), jnp.float32), grad_acc)

    grad_recv = jnp.zeros((token_rows, model_width), jnp.bfloat16)
    attn_zero = (
        jnp.zeros_like(attn_weights[0]),
        jnp.zeros(attn_qkv.shape[1:], jnp.float32),
        jnp.zeros(attn_out.shape[1:], jnp.float32),
        jnp.zeros_like(attn_weights[3]),
    )
    ffn_zero = (
        jnp.zeros_like(ffn_weights[0]),
        jnp.zeros(ffn_up.shape[1:], jnp.float32),
        jnp.zeros_like(ffn_weights[2]),
        jnp.zeros(ffn_down.shape[1:], jnp.float32),
        jnp.zeros_like(ffn_weights[4]),
    )
    grad_acc = (attn_zero, ffn_zero, jnp.zeros_like(end_gain))
    table_acc = jnp.zeros((group_count, model_width), jnp.float32)
    input_all = jnp.zeros((section_count, token_rows, model_width), jnp.bfloat16)
    for tick_index in range(ticks):
        micro_batch = tick_index - (last_section - section_index)
        is_valid = (micro_batch >= 0) & (micro_batch < section_count)
        micro_slot = jnp.clip(micro_batch, 0, section_count - 1)
        live_mask, onehot = micro_inputs(micro_slot)
        hidden_in = lax.dynamic_index_in_dim(kept_inputs, micro_slot, 0, keepdims=False)
        pool_grad = lax.dynamic_index_in_dim(pool_grads, micro_slot, 0, keepdims=False)
        branch_index = jnp.where(is_valid, half_kind, 2)
        d_hidden, grad_acc = lax.switch(
            branch_index,
            [backward_attend, backward_feed, backward_spare],
            hidden_in,
            grad_recv,
            pool_grad,
            live_mask,
            grad_acc,
        )
        at_first = is_valid & (section_index == 0)
        old_input = lax.dynamic_index_in_dim(input_all, micro_slot, 0, keepdims=False)
        input_all = lax.dynamic_update_index_in_dim(
            input_all, jnp.where(at_first, d_hidden.astype(jnp.bfloat16), old_input), micro_slot, 0
        )
        piece_sums = jnp.sum(d_hidden.reshape(entries, pieces_max, model_width), axis=1)
        table_term = lax.dot_general(
            onehot,
            piece_sums,
            (((0,), (0,)), ((), ())),
            precision=HIGH,
            preferred_element_type=jnp.float32,
        )
        table_acc = table_acc + jnp.where(at_first, table_term, 0.0)
        if tick_index < ticks - 1:
            grad_recv = shifted_2(d_hidden.astype(jnp.bfloat16), "section", -1)
    attn_part, ffn_part, end_part = grad_acc
    summed_dp = (
        lax.psum_scatter(attn_part[0], "dp", scatter_dimension=0, tiled=True),
        lax.psum_scatter(attn_part[1], "dp", scatter_dimension=0, tiled=True),
        lax.psum_scatter(attn_part[2], "dp", scatter_dimension=0, tiled=True),
        lax.psum_scatter(attn_part[3], "dp", scatter_dimension=0, tiled=True),
        lax.psum_scatter(ffn_part[0], "dp", scatter_dimension=0, tiled=True),
        lax.psum_scatter(ffn_part[1], "dp", scatter_dimension=0, tiled=True),
        lax.psum_scatter(ffn_part[2], "dp", scatter_dimension=0, tiled=True),
        lax.psum_scatter(ffn_part[3], "dp", scatter_dimension=0, tiled=True),
        lax.psum_scatter(ffn_part[4], "dp", scatter_dimension=0, tiled=True),
        lax.psum_scatter(end_part, "dp", scatter_dimension=0, tiled=True),
        lax.psum_scatter(table_acc, "dp", scatter_dimension=1, tiled=True),
        lax.psum_scatter(pool_term, "dp", scatter_dimension=0, tiled=True),
        lax.psum_scatter(pool_bias_term, "dp", scatter_dimension=0, tiled=True),
    )
    layer_shards = summed_dp[:10]
    table_shard, pool_shard, pool_bias_shard = (summed_dp[10], summed_dp[11], summed_dp[12])

    def place_layer(shard):
        holder = jnp.zeros((layer_count,) + shard.shape, jnp.float32)
        return lax.dynamic_update_index_in_dim(holder, shard, layer_index, 0)

    placed = [place_layer(shard) for shard in layer_shards[:9]]
    totals = (
        lax.psum(placed[0].astype(jnp.bfloat16), "section").astype(jnp.float32),
        lax.psum(placed[1].astype(jnp.bfloat16), "section").astype(jnp.float32),
        lax.psum(placed[2].astype(jnp.bfloat16), "section").astype(jnp.float32),
        lax.psum(placed[3].astype(jnp.bfloat16), "section").astype(jnp.float32),
        lax.psum(placed[4].astype(jnp.bfloat16), "section").astype(jnp.float32),
        lax.psum(placed[5].astype(jnp.bfloat16), "section").astype(jnp.float32),
        lax.psum(placed[6].astype(jnp.bfloat16), "section").astype(jnp.float32),
        lax.psum(placed[7].astype(jnp.bfloat16), "section").astype(jnp.float32),
        lax.psum(placed[8].astype(jnp.bfloat16), "section").astype(jnp.float32),
        lax.psum(layer_shards[9].astype(jnp.bfloat16), "section").astype(jnp.float32),
        lax.psum(table_shard.astype(jnp.bfloat16), "section").astype(jnp.float32),
        lax.psum(pool_shard.astype(jnp.bfloat16), "section").astype(jnp.float32),
        lax.psum(pool_bias_shard.astype(jnp.bfloat16), "section").astype(jnp.float32),
    )
    input_shared = from_root(input_all, "section", 0)
    input_grad = lax.dynamic_index_in_dim(input_shared, section_index, 0, keepdims=False)
    input_grad = input_grad.reshape(entries, pieces_max, model_width)
    return (
        embeddings,
        input_grad,
        totals[10],
        totals[0],
        totals[1],
        totals[2],
        totals[3],
        totals[4],
        totals[5],
        totals[6],
        totals[7],
        totals[8],
        totals[9],
        totals[11],
        totals[12],
    )


def solution(mesh):
    placed = (
        P(("dp", "section"), None, None),
        P(("dp", "section")),
        P(("dp", "section")),
        P(),
        P(),
        P(),
        P(),
        P(),
        P(),
        P(),
        P(),
        P(),
        P(),
        P(),
        P(),
        P(),
        P(("dp", "section"), None),
    )
    return jax.shard_map(
        per_device,
        mesh=mesh,
        in_specs=placed,
        out_specs=(
            P(("dp", "section"), None),
            P(("dp", "section"), None, None),
            P(None, "dp"),
            P(None, "dp"),
            P(None, "dp", None),
            P(None, "dp", None),
            P(None, "dp"),
            P(None, "dp"),
            P(None, "dp", None),
            P(None, "dp"),
            P(None, "dp", None),
            P(None, "dp"),
            P("dp"),
            P("dp", None),
            P("dp"),
        ),
        check_vma=False,
    )
```

profile of v0, /device:TPU:0, one launch (start us, length us, event | category | flops | bytes accessed | tf_op | source)
XLA Modules:
  0.0 1381.6 jit_solution(16096993387324208609)
XLA Ops:
  8.8 6.0 all-gather
  58.3 36.6 %conditional.14 = (bf16[448,512]{1,0:T(8,128)(2,1)}, bf16[64,512]{1,0:T(8,128)(2,1)S(1)}) conditional(s32[]{:T(128)} %clamp.42, (f32[448,512]{1,0:T(8,128)S(1)}, f32[512]{0:T(512)S(1)}, bf16[512,1536]{1,0:T(8,128)(2,1)}, f32[64,7]{1,0:T(8,128)S(1)}, bf16[512,512]{1,0:T(8,128)(2,1)S(1)}, /*index=5*/f32[512]{0:T(512)S(1)}) %tuple.633, ...), branch_computations={%region_0.5_spmd, %region_5.12_spmd, %region_12.13_spmd} | conditional | flops 1944913152 | bytes 18203414 | solution.py:263
  105.7 29.8 %conditional.15 = (bf16[448,512]{1,0:T(8,128)(2,1)}, bf16[64,512]{1,0:T(8,128)(2,1)S(1)}) conditional(s32[]{:T(128)} %clamp.43, (f32[448,512]{1,0:T(8,128)S(1)}, f32[512]{0:T(512)S(1)}, bf16[512,1536]{1,0:T(8,128)(2,1)}, f32[64,7]{1,0:T(8,128)S(1)}, bf16[512,512]{1,0:T(8,128)(2,1)S(1)}, ...), branch_computations={%region_13.18_spmd, %region_18.25_spmd, %region_25.26_spmd} | conditional | flops 1944913152 | bytes 18203414 | solution.py:263
  143.2 30.0 %conditional.16 = (bf16[448,512]{1,0:T(8,128)(2,1)}, bf16[64,512]{1,0:T(8,128)(2,1)S(1)}) conditional(s32[]{:T(128)} %clamp.44, (f32[448,512]{1,0:T(8,128)S(1)}, f32[512]{0:T(512)S(1)}, bf16[512,1536]{1,0:T(8,128)(2,1)}, f32[64,7]{1,0:T(8,128)S(1)}, bf16[512,512]{1,0:T(8,128)(2,1)S(1)}, ...), branch_computations={%region_26.31_spmd, %region_31.38_spmd, %region_38.39_spmd} | conditional | flops 1944913152 | bytes 18203414 | solution.py:263
  181.5 30.0 %conditional.17 = (bf16[448,512]{1,0:T(8,128)(2,1)}, bf16[64,512]{1,0:T(8,128)(2,1)S(1)}) conditional(s32[]{:T(128)} %clamp.45, (f32[448,512]{1,0:T(8,128)S(1)}, f32[512]{0:T(512)S(1)}, bf16[512,1536]{1,0:T(8,128)(2,1)}, f32[64,7]{1,0:T(8,128)S(1)}, bf16[512,512]{1,0:T(8,128)(2,1)S(1)}, ...), branch_computations={%region_39.44_spmd, %region_44.51_spmd, %region_51.52_spmd} | conditional | flops 1944913152 | bytes 18203414 | solution.py:263
  219.3 6.6 conditional.18
  225.9 11.6 collective-permute-start.4
  244.9 10.0 conditional.19
  254.9 10.7 collective-permute-start.5
  265.6 29.6 %all_gather.11 = bf16[256,512]{1,0:T(8,128)(2,1)S(1)} all-gather(bf16[64,512]{1,0:T(8,128)(2,1)S(1)} %copy-done.165), channel_id=1, replica_groups=mesh['dp'=8,'section'=4] {'section'}, dimensions={0}, use_global_device_ids=true | all-gather | bytes 327680 | tf_op jit(solution)/shard_map/all_gather | solution.py:287
  300.8 5.7 dynamic-slice_bitcast_fusion.3
  306.5 18.9 %conditional.21 = (f32[512]{0:T(512)}, f32[512,1536]{1,0:T(8,128)S(1)}, f32[512,512]{1,0:T(8,128)}, f32[512]{0:T(512)S(1)}, f32[512]{0:T(512)}, /*index=5*/f32[5...) conditional(s32[]{:T(128)} %clamp.49, ...), branch_computations={%region_88.98_spmd, %region_98.113_spmd, %region_113.114_spmd} | conditional | flops 5727096320 | bytes 112208368 | solution.py:336
  344.1 12.1 conditional.23
  359.1 146.1 %collective-permute-done.8 = bf16[448,512]{1,0:T(8,128)(2,1)} collective-permute-done((bf16[448,512]{1,0:T(8,128)(2,1)}, bf16[448,512]{1,0:T(8,128)(2,1)}, u32[]{:S(2)}, u32[]{:S(2)}) %collective-permute-start.8) | collective-permute-done | bytes 458784 | tf_op jit(solution)/shard_map/ppermute | solution.py:21
  505.2 66.3 %conditional.24 = (f32[512]{0:T(512)}, f32[512,1536]{1,0:T(8,128)S(1)}, f32[512,512]{1,0:T(8,128)}, f32[512]{0:T(512)S(1)}, f32[512]{0:T(512)}, /*index=5*/f32[5...) conditional(s32[]{:T(128)} %clamp.52, (f32[448,512]{1,0:T(8,128)}, ...), branch_computations={%region_168.179_spmd, %region_179.194_spmd, %region_194.195_spmd} | conditional | flops 5729197056 | bytes 124284528 | solution.py:336
  574.4 8.4 collective-permute-done.9
  582.8 66.3 %conditional.25 = (f32[512]{0:T(512)}, f32[512,1536]{1,0:T(8,128)S(1)}, f32[512,512]{1,0:T(8,128)}, f32[512]{0:T(512)S(1)}, f32[512]{0:T(512)}, /*index=5*/f32[5...) conditional(s32[]{:T(128)} %clamp.53, (f32[448,512]{1,0:T(8,128)}, ...), branch_computations={%region_195.206_spmd, %region_206.221_spmd, %region_221.222_spmd} | conditional | flops 5729197056 | bytes 124284528 | solution.py:336
  606.1 5.3 fusion.791
  651.9 13.2 conditional.20
  666.0 62.1 %conditional.26 = (f32[512]{0:T(512)}, f32[512,1536]{1,0:T(8,128)S(1)}, f32[512,512]{1,0:T(8,128)}, f32[512]{0:T(512)S(1)}, f32[512]{0:T(512)}, /*index=5*/f32[5...) conditional(s32[]{:T(128)} %clamp.54, (f32[448,512]{1,0:T(8,128)}, ...), branch_computations={%region_222.233_spmd, %region_233.248_spmd, %region_248.249_spmd} | conditional | flops 5729197056 | bytes 124284528 | solution.py:336
  731.6 10.7 collective-permute-done.11
  742.3 58.1 %conditional.27 = (f32[512]{0:T(512)}, f32[512,1536]{1,0:T(8,128)}, f32[512,512]{1,0:T(8,128)}, f32[512]{0:T(512)S(1)}, f32[512]{0:T(512)}, /*index=5*/f32[512,2...) conditional(s32[]{:T(128)} %clamp.55, (f32[448,512]{1,0:T(8,128)}, ...), branch_computations={%region_249.260_spmd, %region_260.275_spmd, %region_275.276_spmd} | conditional | flops 5729197056 | bytes 137391712 | solution.py:336
  763.6 5.3 fusion.797
  813.0 51.9 %reduce-scatter.11.cloned.1.call-done = f32[64,512]{1,0:T(8,128)} async-done(((f32[512,512]{1,0:T(8,128)}), f32[64,512]{1,0:T(8,128)}) %reduce-scatter.11.cloned.1.call-update) | async-done | bytes 131088 | tf_op jit(solution)/shard_map/reduce_scatter | solution.py:365
  865.9 89.5 %reduce-scatter.17.cloned.1.call-done = f32[64,2048]{1,0:T(8,128)} async-done(((f32[512,2048]{1,0:T(8,128)}), f32[64,2048]{1,0:T(8,128)}) %reduce-scatter.17.cloned.1.call-update) | async-done | bytes 524304 | tf_op jit(solution)/shard_map/reduce_scatter | solution.py:374
  957.2 76.3 %reduce-scatter.9.cloned.1.call-done = f32[64,1536]{1,0:T(8,128)} async-done(((f32[512,1536]{1,0:T(8,128)}), f32[64,1536]{1,0:T(8,128)}) %reduce-scatter.9.cloned.1.call-update) | async-done | bytes 393232 | tf_op jit(solution)/shard_map/reduce_scatter | solution.py:364
  1036.0 88.5 %reduce-scatter.13.cloned.1.call-done = f32[64,2048]{1,0:T(8,128)} async-done(((f32[512,2048]{1,0:T(8,128)}), f32[64,2048]{1,0:T(8,128)}) %reduce-scatter.13.cloned.1.call-update) | async-done | bytes 524304 | tf_op jit(solution)/shard_map/reduce_scatter | solution.py:368
  1125.6 90.2 %reduce-scatter.15.cloned.1.call-done = f32[256,512]{1,0:T(8,128)} async-done(((f32[2048,512]{1,0:T(8,128)}), f32[256,512]{1,0:T(8,128)}) %reduce-scatter.15.cloned.1.call-update) | async-done | bytes 524304 | tf_op jit(solution)/shard_map/reduce_scatter | solution.py:370
  1221.7 36.7 %all-reduce.7 = (bf16[512]{0:T(512)(128)(2,1)S(1)}, bf16[512]{0:T(512)(128)(2,1)S(1)}, bf16[512]{0:T(512)(128)(2,1)S(1)}, f32[2048]{0:T(1024)S(1)}, bf16[512]{0:...) all-reduce(f32[512]{0:T(512)} %get-tuple-element.2273, ...), channel_id=3, replica_groups=mesh['dp'=8,'section'=4] {'dp'}, use_global_device_ids=true, to_apply=%region_279.280.clone | all-reduce | flops 6656 | bytes 44032
  1259.1 22.0 %reduce-scatter.19.cloned.1.call-done = f32[64,8]{1,0:T(8,128)} async-done(((f32[512,8]{1,0:T(8,128)}), f32[64,8]{1,0:T(8,128)}) %reduce-scatter.19.cloned.1.call-update) | async-done | bytes 2064
  1281.9 5.7 all-reduce.8
  1292.2 70.0 %all-reduce.15.cloned.1.call-done = (bf16[4,448,512]{2,1,0:T(8,128)(2,1)}, bf16[2,64,1536]{2,1,0:T(8,128)(2,1)}, bf16[2,64,512]{2,1,0:T(8,128)(2,1)}, bf16[2,64,...) async-done(((bf16[4,448,512]{2,1,0:T(8,128)(2,1)}, bf16[2,64,1536]{2,1,0:T(8,128)(2,1)}, bf16[2,64,512]{2,1,0:T(8,128)(2,1)}, ...) | async-done | bytes 3670032 | tf_op jit(solution)/shard_map/psum | solution.py:26
  (709 shorter events, 513.7 us)
Async XLA Ops:
  7.2 41.0 %all-gather.3.cloned.1.call-start = ((), (), s32[]{:S(2)}) async-start(), calls=%async_computation.6 | async-start | bytes 2293760 | tf_op jit(solution)/shard_map/all_gather | solution.py:199
  7.9 792.6 %all-reduce.13.cloned.1.call-start = ((), (), s32[]{:S(2)}) async-start(), calls=%async_computation.7 | async-start | bytes 524288 | tf_op jit(solution)/shard_map/psum | solution.py:26
  58.3 41.4 %copy-start.97 = (bf16[1,64,7,512]{3,1,0,2:T(8,128)(2,1)S(1)}, bf16[1,64,7,512]{3,1,0,2:T(8,128)(2,1)}, u32[]{:S(2)}) copy-start(bf16[1,64,7,512]{3,1,0,2:T(8,128)(2,1)} %get-tuple-element.2787) | copy-start | bytes 1376260
  94.9 6.8 collective-permute-start
  135.5 5.0 collective-permute-start.1
  173.2 5.6 collective-permute-start.2
  211.6 5.1 collective-permute-start.3
  225.9 16.4 %collective-permute-start.4 = (bf16[448,512]{1,0:T(8,128)(2,1)}, bf16[448,512]{1,0:T(8,128)(2,1)}, u32[]{:S(2)}, u32[]{:S(2)}) collective-permute-start(bf16[448,512]{1,0:T(8,128)(2,1)} %get-tuple-element.2196), channel_id=1, source_target_pairs={{0,1},{1,2},{2,3},{4,5},{5,6},{6,7},{8,9},{9,10},{10,11},{12,13},{... | collective-permute-start | bytes 1376264 | tf_op jit(solution)/shard_map/ppermute | solution.py:21
  244.9 50.3 %copy-start.92 = (bf16[1,64,7,512]{3,1,0,2:T(8,128)(2,1)S(1)}, bf16[1,64,7,512]{3,1,0,2:T(8,128)(2,1)}, u32[]{:S(2)}) copy-start(bf16[1,64,7,512]{3,1,0,2:T(8,128)(2,1)} %get-tuple-element.2783) | copy-start | bytes 1376260
  254.9 45.9 %copy-start.169 = (bf16[64,512]{1,0:T(8,128)(2,1)}, bf16[64,512]{1,0:T(8,128)(2,1)S(1)}, u32[]{:S(2)}) copy-start(bf16[64,512]{1,0:T(8,128)(2,1)S(1)} %get-tuple-element.2197) | copy-start | bytes 196612
  254.9 42.9 %copy-start.55 = (f32[448,512]{1,0:T(8,128)S(1)}, f32[448,512]{1,0:T(8,128)}, u32[]{:S(2)}) copy-start(f32[448,512]{1,0:T(8,128)} %add.1525) | copy-start | bytes 2752516
  254.9 42.9 %collective-permute-start.5 = (bf16[448,512]{1,0:T(8,128)(2,1)}, bf16[448,512]{1,0:T(8,128)(2,1)}, u32[]{:S(2)}, u32[]{:S(2)}) collective-permute-start(bf16[448,512]{1,0:T(8,128)(2,1)} %get-tuple-element.2198), channel_id=1, source_target_pairs={{0,1},{1,2},{2,3},{4,5},{5,6},{6,7},{8,9},{9,10},{10,11},{12,13},{... | collective-permute-start | bytes 1376264 | tf_op jit(solution)/shard_map/ppermute | solution.py:21
  325.4 6.1 collective-permute-start.6
  336.4 7.7 collective-permute-start.7
  356.2 149.0 %copy-start.130 = (f32[64,512]{1,0:T(8,128)}, f32[64,512]{1,0:T(8,128)S(1)}, u32[]{:S(2)}) copy-start(f32[64,512]{1,0:T(8,128)S(1)} %get-tuple-element.2268) | copy-start | bytes 393220
  356.2 149.0 %collective-permute-start.8 = (bf16[448,512]{1,0:T(8,128)(2,1)}, bf16[448,512]{1,0:T(8,128)(2,1)}, u32[]{:S(2)}, u32[]{:S(2)}) collective-permute-start(bf16[448,512]{1,0:T(8,128)(2,1)} %get-tuple-element.2221), channel_id=1, source_target_pairs={{1,0},{2,1},{3,2},{5,4},{6,5},{7,6},{9,8},{10,9},{11,10},{13,12},{... | collective-permute-start | bytes 1376264 | tf_op jit(solution)/shard_map/ppermute | solution.py:21
  571.5 11.3 collective-permute-start.9
  649.1 16.9 %collective-permute-start.10 = (bf16[448,512]{1,0:T(8,128)(2,1)}, bf16[448,512]{1,0:T(8,128)(2,1)}, u32[]{:S(2)}, u32[]{:S(2)}) collective-permute-start(bf16[448,512]{1,0:T(8,128)(2,1)} %get-tuple-element.2243), channel_id=1, source_target_pairs={{1,0},{2,1},{3,2},{5,4},{6,5},{7,6},{9,8},{10,9},{11,10},{13,12},{... | collective-permute-start | bytes 1376264 | tf_op jit(solution)/shard_map/ppermute | solution.py:21
  728.2 14.2 %collective-permute-start.11 = (bf16[448,512]{1,0:T(8,128)(2,1)}, bf16[448,512]{1,0:T(8,128)(2,1)}, u32[]{:S(2)}, u32[]{:S(2)}) collective-permute-start(bf16[448,512]{1,0:T(8,128)(2,1)} %get-tuple-element.2254), channel_id=1, source_target_pairs={{1,0},{2,1},{3,2},{5,4},{6,5},{7,6},{9,8},{10,9},{11,10},{13,12},{... | collective-permute-start | bytes 1376264 | tf_op jit(solution)/shard_map/ppermute | solution.py:21
  730.2 134.7 %reduce-scatter.11.cloned.1.call-start = ((), (), s32[]{:S(2)}) async-start(), calls=%async_computation.9 | async-start | bytes 1179648 | tf_op jit(solution)/shard_map/reduce_scatter | solution.py:365
  742.3 58.2 %copy-start.59 = (bf16[64,2048]{1,0:T(8,128)(2,1)S(1)}, bf16[64,2048]{1,0:T(8,128)(2,1)}, u32[]{:S(2)}) copy-start(bf16[64,2048]{1,0:T(8,128)(2,1)} %param.75) | copy-start | bytes 786436
  800.5 154.9 %reduce-scatter.17.cloned.1.call-start = ((), (), s32[]{:S(2)}) async-start(), calls=%async_computation.12 | async-start | bytes 4718592 | tf_op jit(solution)/shard_map/reduce_scatter | solution.py:374
  804.1 229.4 %reduce-scatter.9.cloned.1.call-start = ((), (), s32[]{:S(2)}) async-start(), calls=%async_computation.8 | async-start | bytes 3538944 | tf_op jit(solution)/shard_map/reduce_scatter | solution.py:364
  804.7 319.7 %reduce-scatter.13.cloned.1.call-start = ((), (), s32[]{:S(2)}) async-start(), calls=%async_computation.10 | async-start | bytes 4718592 | tf_op jit(solution)/shard_map/reduce_scatter | solution.py:368
  805.3 410.5 %reduce-scatter.15.cloned.1.call-start = ((), (), s32[]{:S(2)}) async-start(), calls=%async_computation.11 | async-start | bytes 4718592 | tf_op jit(solution)/shard_map/reduce_scatter | solution.py:370
  806.0 475.1 %reduce-scatter.19.cloned.1.call-start = ((), (), s32[]{:S(2)}) async-start(), calls=%async_computation.13 | async-start | bytes 294912
  813.0 549.2 %all-reduce.15.cloned.1.call-start = ((), (), s32[]{:S(2)}) async-start(), calls=%async_computation.14 | async-start | bytes 7340032 | tf_op jit(solution)/shard_map/psum | solution.py:26
  865.9 351.0 %copy-start.142 = (bf16[2,64,512]{2,1,0:T(8,128)(2,1)}, bf16[2,64,512]{2,1,0:T(8,128)(2,1)S(1)}, u32[]{:S(2)}) copy-start(bf16[2,64,512]{2,1,0:T(8,128)(2,1)S(1)} %bitcast_dynamic-update-slice_fusion.16) | copy-start | bytes 393220
  1034.2 183.5 %copy-start.209 = (bf16[2048]{0:T(1024)(128)(2,1)S(1)}, bf16[2048]{0:T(1024)(128)(2,1)}, u32[]{:S(2)}) copy-start(bf16[2048]{0:T(1024)(128)(2,1)} %param.74) | copy-start | bytes 12292
  1034.2 183.5 %copy-start.232 = (u32[32]{0:T(128)S(1)}, u32[32]{0:T(128)}, u32[]{:S(2)}) copy-start(u32[32]{0:T(128)} %constant.2268) | copy-start | bytes 388
  1036.0 183.7 %copy-start.19 = (bf16[512,2048]{1,0:T(8,128)(2,1)S(1)}, bf16[512,2048]{1,0:T(8,128)(2,1)}, u32[]{:S(2)}) copy-start(bf16[512,2048]{1,0:T(8,128)(2,1)} %param.73) | copy-start | bytes 6291460
  1125.6 91.3 %copy-start.60 = (bf16[2,64,2048]{2,1,0:T(8,128)(2,1)}, bf16[2,64,2048]{2,1,0:T(8,128)(2,1)S(1)}, u32[]{:S(2)}) copy-start(bf16[2,64,2048]{2,1,0:T(8,128)(2,1)S(1)} %bitcast_dynamic-update-slice_fusion.7) | copy-start | bytes 1572868
  (123 other events, 821.9 us)
Sparse Core Ops, SparseCore 0:
  9.6 23.8 all-gather.2
  730.3 45.0 all-reduce.12
  800.6 64.2 reduce-scatter.10
  868.4 86.9 reduce-scatter.16
  959.2 74.1 reduce-scatter.8
  1037.4 87.0 reduce-scatter.12
  1128.1 87.6 reduce-scatter.14
  1220.0 61.0 reduce-scatter.18
  1285.2 76.9 all-reduce.14
where the time goes:
time: 1390 us; the launch traced here: 1380 us
  waiting for transfers between devices  661 us (48%)
  local copies, waits for them, and re-layouts  228 us (16%)
  matrix products  162 us (12%)
  other arithmetic  112 us (8%)
  loops' own time  85.8 us (6%)
  blocking collectives  78 us (6%)
  starting transfers between devices  39.1 us (3%)
  between operations  16.7 us (1%)
    ppermute x12, waiting for transfers between devices, shifted_2(): return lax.ppermute(block, axis, route)  170 us
    reduce_scatter x1, waiting for transfers between devices, per_device(): lax.psum_scatter(ffn_part[3], 'dp', scatter_dimension=0, tiled=True)  90.2 us
    reduce_scatter x1, waiting for transfers between devices, per_device(): lax.psum_scatter(pool_term, 'dp', scatter_dimension=0, tiled=True)  89.5 us
    reduce_scatter x1, waiting for transfers between devices, per_device(): lax.psum_scatter(ffn_part[1], 'dp', scatter_dimension=0, tiled=True)  88.5 us
    reduce_scatter x1, waiting for transfers between devices, per_device(): lax.psum_scatter(attn_part[1], 'dp', scatter_dimension=0, tiled=True)  76.3 us
    psum x2, waiting for transfers between devices, from_root(): return lax.psum(jnp.where(mine, array, jnp.zeros_like(array)), axis)  70 us
    another operation x7, loops' own time, per_device(): lax.switch(branch_index, [forward_attend, forward_feed, forward_spare], h...  59.1 us
    reduce_scatter x1, waiting for transfers between devices, per_device(): lax.psum_scatter(attn_part[2], 'dp', scatter_dimension=0, tiled=True)  51.9 us
  transfers between devices with their start and end apart: 21, of which 12 were waited for; matrix products, arithmetic and copies ran while one was open for 11% of the time, Pallas kernels for 0%

commit v1 on v0

v1 whole, which is shorter than its diff:
```python
import jax
import jax.numpy as jnp
from jax import lax
from jax.sharding import PartitionSpec as P

HEADS = 8


EPS = 1e-05
MASKED = -1e30
HIGH = lax.Precision.HIGHEST


def layer_norm(values, norm_gain):
    centre = values - jnp.mean(values, axis=-1, keepdims=True)
    spread = jnp.mean(centre * centre, axis=-1, keepdims=True)
    return centre * lax.rsqrt(spread + EPS) * norm_gain


def pool_mean(hidden, live_mask, norm_gain):
    entries, pieces = live_mask.shape
    normed = layer_norm(hidden, norm_gain).reshape(entries, pieces, -1)
    return jnp.sum(normed * live_mask[:, :, None], axis=1) / jnp.sum(
        live_mask, axis=1, keepdims=True
    )


def matmul_plain(left_side, right_side):
    return jnp.dot(left_side, right_side, preferred_element_type=jnp.float32)


def matmul_left(left_side, right_side):
    return lax.dot_general(
        left_side, right_side, (((0,), (0,)), ((), ())), preferred_element_type=jnp.float32
    )


def matmul_right(left_side, right_side):
    return lax.dot_general(
        left_side, right_side, (((1,), (1,)), ((), ())), preferred_element_type=jnp.float32
    )


def gelu_exact(values):
    return jax.nn.gelu(values, approximate=False)


def attend_forward(hidden, live_mask, weights):
    norm_gain, w_qkv, w_out, b_out = weights
    entries, pieces = live_mask.shape
    model_width = hidden.shape[1]
    head_size = model_width // HEADS
    normed, norm_back = jax.vjp(layer_norm, hidden, norm_gain)
    normed_low = normed.astype(jnp.bfloat16)
    projected = matmul_plain(normed_low, w_qkv).astype(jnp.bfloat16)
    projected = projected.reshape(entries, pieces, 3, HEADS, head_size)
    queries = projected[:, :, 0]
    key_rows = projected[:, :, 1]
    value_rows = projected[:, :, 2]
    scores = jnp.einsum(
        "eqhd,ekhd->ehqk", queries, key_rows, preferred_element_type=jnp.float32
    ) * head_size ** (-0.5)
    scores = jnp.where(live_mask[:, None, None, :] > 0.5, scores, MASKED)
    shifted = jnp.exp(scores - jnp.max(scores, axis=-1, keepdims=True))
    attention = shifted / jnp.sum(shifted, axis=-1, keepdims=True)
    attention_low = attention.astype(jnp.bfloat16)
    context = jnp.einsum(
        "ehqk,ekhd->eqhd", attention_low, value_rows, preferred_element_type=jnp.float32
    )
    context = context.astype(jnp.bfloat16).reshape(entries * pieces, model_width)
    section_out = (hidden + matmul_plain(context, w_out) + b_out).astype(jnp.bfloat16)
    saved_state = (
        norm_back,
        normed_low,
        queries,
        key_rows,
        value_rows,
        attention,
        attention_low,
        context,
    )
    return (section_out, saved_state)


def attend_backward(saved_state, grad_low, live_mask, weights, grad_acc):
    norm_gain, w_qkv, w_out, b_out = weights
    entries, pieces = live_mask.shape
    model_width = w_out.shape[0]
    head_size = model_width // HEADS
    norm_back, normed_low, queries, key_rows, value_rows, attention, attention_low, context = (
        saved_state
    )
    gain_sum, qkv_sum, out_sum, bias_sum = grad_acc
    grad_wide = grad_low.astype(jnp.float32)
    out_sum = out_sum + matmul_left(context, grad_low)
    bias_sum = bias_sum + jnp.sum(grad_wide, axis=0)
    d_context = (
        matmul_right(grad_low, w_out)
        .astype(jnp.bfloat16)
        .reshape(entries, pieces, HEADS, head_size)
    )
    d_attention = jnp.einsum(
        "eqhd,ekhd->ehqk", d_context, value_rows, preferred_element_type=jnp.float32
    )
    d_values = jnp.einsum(
        "ehqk,eqhd->ekhd", attention_low, d_context, preferred_element_type=jnp.float32
    )
    d_scores = attention * (d_attention - jnp.sum(attention * d_attention, axis=-1, keepdims=True))
    d_scores = d_scores.astype(jnp.bfloat16)
    d_queries = jnp.einsum(
        "ehqk,ekhd->eqhd", d_scores, key_rows, preferred_element_type=jnp.float32
    ) * head_size ** (-0.5)
    d_keys = jnp.einsum(
        "ehqk,eqhd->ekhd", d_scores, queries, preferred_element_type=jnp.float32
    ) * head_size ** (-0.5)
    d_projected = jnp.stack([d_queries, d_keys, d_values], axis=2).astype(jnp.bfloat16)
    d_projected = d_projected.reshape(entries * pieces, 3 * model_width)
    qkv_sum = qkv_sum + matmul_left(normed_low, d_projected)
    d_hidden, gain_term = norm_back(matmul_right(d_projected, w_qkv))
    return (d_hidden + grad_wide, (gain_sum + gain_term, qkv_sum, out_sum, bias_sum))


def feed_forward(hidden, weights):
    norm_gain, w_up, b_up, w_down, b_down = weights
    normed, norm_back = jax.vjp(layer_norm, hidden, norm_gain)
    normed_low = normed.astype(jnp.bfloat16)
    inner_act = matmul_plain(normed_low, w_up) + b_up
    activated, gelu_back = jax.vjp(gelu_exact, inner_act)
    activated_low = activated.astype(jnp.bfloat16)
    section_out = (hidden + matmul_plain(activated_low, w_down) + b_down).astype(jnp.bfloat16)
    return (section_out, (norm_back, normed_low, gelu_back, activated_low))


def feed_backward(grad_low, saved_state, weights, grad_acc):
    norm_gain, w_up, b_up, w_down, b_down = weights
    norm_back, normed_low, gelu_back, activated_low = saved_state
    gain_sum, up_sum, up_bias_sum, down_sum, down_bias_sum = grad_acc
    grad_wide = grad_low.astype(jnp.float32)
    down_sum = down_sum + matmul_left(activated_low, grad_low)
    down_bias_sum = down_bias_sum + jnp.sum(grad_wide, axis=0)
    d_inner = gelu_back(matmul_right(grad_low, w_down))[0].astype(jnp.bfloat16)
    up_sum = up_sum + matmul_left(normed_low, d_inner)
    up_bias_sum = up_bias_sum + jnp.sum(d_inner.astype(jnp.float32), axis=0)
    d_hidden, gain_term = norm_back(matmul_right(d_inner, w_up))
    return (
        d_hidden + grad_wide,
        (gain_sum + gain_term, up_sum, up_bias_sum, down_sum, down_bias_sum),
    )


def per_device(
    pieces,
    counts,
    groups,
    group_table,
    attn_gain,
    attn_qkv,
    attn_out,
    attn_bias,
    ffn_gain,
    ffn_up,
    ffn_up_bias,
    ffn_down,
    ffn_down_bias,
    final_gain,
    pool_weight,
    pool_bias,
    emb_cotangent,
):
    entries, pieces_max, model_width = pieces.shape
    token_rows = entries * pieces_max
    group_count = group_table.shape[0]
    layer_count = attn_qkv.shape[0]
    wide = lambda a: a.astype(jnp.float32)
    live_mask = wide(lax.broadcasted_iota(jnp.int32, (entries, pieces_max), 1) < counts[:, None])
    onehot = wide(groups[:, None] == lax.broadcasted_iota(jnp.int32, (entries, group_count), 1))
    group_rows = matmul_plain(onehot.astype(jnp.bfloat16), group_table)
    hidden = (wide(pieces) + group_rows[:, None, :]).reshape(token_rows, model_width)
    saved = []
    for layer in range(layer_count):
        attn_weights = (wide(attn_gain[layer]), attn_qkv[layer], attn_out[layer], wide(attn_bias[layer]))
        ffn_weights = (
            wide(ffn_gain[layer]),
            ffn_up[layer],
            wide(ffn_up_bias[layer]),
            ffn_down[layer],
            wide(ffn_down_bias[layer]),
        )
        middle, attn_state = attend_forward(hidden, live_mask, attn_weights)
        after, ffn_state = feed_forward(wide(middle), ffn_weights)
        saved.append((hidden, attn_state, attn_weights, ffn_state, ffn_weights))
        hidden = wide(after)
    pooled_wide, pool_back = jax.vjp(
        lambda values, gain: pool_mean(values, live_mask, gain), hidden, wide(final_gain)
    )
    pooled = pooled_wide.astype(jnp.bfloat16)
    embeddings = (matmul_plain(pooled, pool_weight) + wide(pool_bias)).astype(jnp.bfloat16)
    pool_term = matmul_left(pooled, emb_cotangent)
    pool_bias_term = jnp.sum(wide(emb_cotangent), axis=0)
    d_pooled = matmul_right(emb_cotangent, pool_weight).astype(jnp.bfloat16)
    d_hidden, end_term = pool_back(wide(d_pooled))

    def reduced(term, dim):
        part = lax.psum_scatter(term.astype(jnp.bfloat16), "dp", scatter_dimension=dim, tiled=True)
        return wide(lax.psum(part, "section"))

    layer_terms = [None] * layer_count
    for layer in reversed(range(layer_count)):
        hidden_in, attn_state, attn_weights, ffn_state, ffn_weights = saved[layer]
        zeros5 = (0.0,) * 5
        d_hidden, ffn_terms = feed_backward(
            d_hidden.astype(jnp.bfloat16), ffn_state, ffn_weights, zeros5
        )
        d_hidden, attn_terms = attend_backward(
            attn_state, d_hidden.astype(jnp.bfloat16), live_mask, attn_weights, (0.0,) * 4
        )
        layer_terms[layer] = tuple(attn_terms) + tuple(ffn_terms)
    input_grad = d_hidden.astype(jnp.bfloat16).reshape(entries, pieces_max, model_width)
    piece_sums = jnp.sum(d_hidden.reshape(entries, pieces_max, model_width), axis=1)
    table_term = lax.dot_general(
        onehot, piece_sums, (((0,), (0,)), ((), ())), precision=HIGH, preferred_element_type=jnp.float32
    )
    stacked = [jnp.stack([terms[k] for terms in layer_terms]) for k in range(9)]
    totals = [reduced(term, 1) for term in stacked]
    return (
        embeddings,
        input_grad,
        reduced(table_term, 1),
        *totals,
        reduced(end_term, 0),
        reduced(pool_term, 0),
        reduced(pool_bias_term, 0),
    )


def solution(mesh):
    placed = (
        P(("dp", "section"), None, None),
        P(("dp", "section")),
        P(("dp", "section")),
        P(),
        P(),
        P(),
        P(),
        P(),
        P(),
        P(),
        P(),
        P(),
        P(),
        P(),
        P(),
        P(),
        P(("dp", "section"), None),
    )
    return jax.shard_map(
        per_device,
        mesh=mesh,
        in_specs=placed,
        out_specs=(
            P(("dp", "section"), None),
            P(("dp", "section"), None, None),
            P(None, "dp"),
            P(None, "dp"),
            P(None, "dp", None),
            P(None, "dp", None),
            P(None, "dp"),
            P(None, "dp"),
            P(None, "dp", None),
            P(None, "dp"),
            P(None, "dp", None),
            P(None, "dp"),
            P("dp"),
            P("dp", None),
            P("dp"),
        ),
        check_vma=False,
    )
```

time: 1390 us -> 1000 us (0.72)
  local copies, waits for them, and re-layouts: 228 us -> 71.1 us
  loops' own time: 85.8 us -> 0 us
  waiting for transfers between devices: 661 us -> 726 us
  other arithmetic: 112 us -> 51 us
  matrix products: 162 us -> 102 us
  blocking collectives: 78 us -> 26.2 us
  starting transfers between devices: 39.1 us -> 0.71 us
    unnamed x10 -> x18, waiting for transfers between devices: 24.5 us -> 355 us
    ppermute x12 -> x0, waiting for transfers between devices: 170 us -> none  [shifted_2(): return lax.ppermute(block, axis, route)]
    another operation x14 -> x0, loops' own time: 85.8 us -> none  [the longest x7 59.1 us: per_device(): lax.switch(branch_index, [forward_attend, forward_feed, forward_spare], h...]
    reduce_scatter x5, waiting for transfers between devices: 396 us -> 332 us  [reduced(): lax.psum_scatter(term.astype(jnp.bfloat16), 'dp', scatter_dimension=dim,...]
    ppermute x12 -> x0, starting transfers between devices: 38.6 us -> none  [shifted_2(): return lax.ppermute(block, axis, route)]
    all_gather x2 -> x0, blocking collectives: 35.6 us -> none  [the longest x1 29.6 us: per_device(): lax.all_gather(own_pool_grad, 'section', axis=0, tiled=True)]
    psum x2 -> x1, waiting for transfers between devices: 70 us -> 38.4 us  [reduced(): return wide(lax.psum(part, 'section'))]
    reshape x8 -> x2, local copies, waits for them, and re-layouts: 35.4 us -> 9.62 us  [attend_forward(): projected = projected.reshape(entries, pieces, 3, HEADS, head_size)]
  transfers between devices with their start and end apart: 21 -> 12, of which waited for: 12 -> 12; matrix products, arithmetic and copies ran while one was open for 11% -> 7% of each run, Pallas kernels for 0% -> 0%
where the time goes in v1:
time: 1000 us; the launch traced here: 993 us
  waiting for transfers between devices  726 us (73%)
  matrix products  102 us (10%)
  local copies, waits for them, and re-layouts  71.1 us (7%)
  other arithmetic  51 us (5%)
  blocking collectives  26.2 us (3%)
  between operations  17 us (2%)
    unnamed x18, waiting for transfers between devices  355 us
    reduce_scatter x5, waiting for transfers between devices, reduced(): lax.psum_scatter(term.astype(jnp.bfloat16), 'dp', scatter_dimension=dim,...  332 us
    psum x1, waiting for transfers between devices, reduced(): return wide(lax.psum(part, 'section'))  38.4 us
    dot_general x10, matrix products, matmul_plain(): return jnp.dot(left_side, right_side, preferred_element_type=jnp.float32)  35.6 us
    dot_general x9, matrix products, matmul_right(): lax.dot_general(left_side, right_side, (((1,), (1,)), ((), ())), preferre...  22.7 us
    unnamed x1, blocking collectives  20.4 us
  transfers between devices with their start and end apart: 12, of which 12 were waited for; matrix products, arithmetic and copies ran while one was open for 7% of the time, Pallas kernels for 0%

profile of v1, /device:TPU:0, one launch (start us, length us, event | category | flops | bytes accessed | tf_op | source)
XLA Modules:
  0.0 993.4 jit_solution(13084185245794083068)
XLA Ops:
  25.1 3.6 convolution_convert_fusion.8
  28.6 5.0 reshape.335
  33.6 3.4 fusion.194
  37.0 4.6 fusion.195
  41.5 2.8 fusion.77
  49.9 12.0 %multiply_convert_fusion.1 = (bf16[448,2048]{1,0:T(8,128)(2,1)S(1)}, f32[448,2048]{1,0:T(8,128)}, f32[448,2048]{1,0:T(8,128)}) fusion(f32[2048]{0:T(1024)S(1)} %bitcast.272, bf16[2,512,2048]{2,1,0:T(8,128)(2,1)} %param.26, bf16[448,512]{1,0:T(8,128)(2,1)S(1)} %get-tuple-element.144, f32[512]{0:T(512)S(1)} %bitcast.256, f32[448]{0:T(512)S(1)} %fusion.166, ...), kind=kOutput, calls=%fused_computation.24 | convolution fusion | flops 1001226240 | bytes 11744768 | tf_op jit(solution)/shard_map/dot_general | solution.py:29
  66.8 4.6 reshape.337
  71.4 3.5 fusion.193
  74.9 5.0 fusion.196
  89.9 10.5 %multiply_convert_fusion = (bf16[448,2048]{1,0:T(8,128)(2,1)S(1)}, f32[448,2048]{1,0:T(8,128)S(1)}, f32[448,2048]{1,0:T(8,128)S(1)}) fusion(f32[2048]{0:T(1024)} %bitcast.274, bf16[2,512,2048]{2,1,0:T(8,128)(2,1)} %param.26, bf16[448,512]{1,0:T(8,128)(2,1)} %copy-done.9, f32[512]{0:T(512)S(1)} %bitcast.261, f32[448]{0:T(512)S(1)} %fusion.168, ...), kind=kOutput, calls=%fused_computation.11 | convolution fusion | flops 1001226240 | bytes 11744768 | tf_op jit(solution)/shard_map/dot_general | solution.py:29
  105.3 3.3 fusion.198
  127.4 4.9 convert_element_type.315
  132.4 3.0 fusion.141
  136.9 4.8 fusion.199
  158.5 2.7 fusion.126
  169.0 4.6 convert_element_type.323
  179.5 3.1 fusion.15
  187.3 2.9 fusion.17
  195.2 3.8 multiply_reduce_fusion.4
  213.9 70.8 %reduce-scatter.32.cloned.1.call-done = bf16[64,2048]{1,0:T(8,128)(2,1)} async-done(((bf16[512,2048]{1,0:T(8,128)(2,1)}), bf16[64,2048]{1,0:T(8,128)(2,1)}) %reduce-scatter.32.cloned.1.call-update) | async-done | bytes 262160 | tf_op jit(solution)/shard_map/reduce_scatter | solution.py:204
  284.6 77.3 %reduce-scatter.24.cloned.1.call-done = bf16[2,64,1536]{2,1,0:T(8,128)(2,1)} async-done(((bf16[2,512,1536]{2,1,0:T(8,128)(2,1)}), bf16[2,64,1536]{2,1,0:T(8,128)(2,1)}) %reduce-scatter.24.cloned.1.call-update) | async-done | bytes 393232 | tf_op jit(solution)/shard_map/reduce_scatter | solution.py:204
  362.0 90.9 %reduce-scatter.28.cloned.1.call-done = bf16[2,64,2048]{2,1,0:T(8,128)(2,1)} async-done(((bf16[2,512,2048]{2,1,0:T(8,128)(2,1)}), bf16[2,64,2048]{2,1,0:T(8,128)(2,1)}) %reduce-scatter.28.cloned.1.call-update) | async-done | bytes 524304 | tf_op jit(solution)/shard_map/reduce_scatter | solution.py:204
  452.9 91.2 %reduce-scatter.30.cloned.1.call-done = bf16[2,256,512]{2,1,0:T(8,128)(2,1)} async-done(((bf16[2,2048,512]{2,1,0:T(8,128)(2,1)}), bf16[2,256,512]{2,1,0:T(8,128)(2,1)}) %reduce-scatter.30.cloned.1.call-update) | async-done | bytes 524304 | tf_op jit(solution)/shard_map/reduce_scatter | solution.py:204
  547.2 20.4 %all-reduce.2 = (bf16[512]{0:T(512)(128)(2,1)S(1)}, bf16[2048]{0:T(1024)(128)(2,1)S(1)}) all-reduce(bf16[512]{0:T(512)(128)(2,1)S(1)} %copy-done.62, bf16[2048]{0:T(1024)(128)(2,1)S(1)} %reduce_sum.452), channel_id=12, replica_groups=mesh['dp'=8,'section'=4] {'dp'}, use_global_device_ids=true, to_apply=%region_60.61.clone | all-reduce | flops 2560 | bytes 10240
  569.0 39.2 %reduce-scatter.36.cloned.1.call-done = bf16[64,2]{1,0:T(8,128)(2,1)} async-done(((bf16[512,2]{1,0:T(8,128)(2,1)}), bf16[64,2]{1,0:T(8,128)(2,1)}) %reduce-scatter.36.cloned.1.call-update) | async-done | bytes 272
  609.0 62.8 %reduce-scatter.38.cloned.1.call-done = bf16[64,2]{1,0:T(8,128)(2,1)} async-done(((bf16[512,2]{1,0:T(8,128)(2,1)}), bf16[64,2]{1,0:T(8,128)(2,1)}) %reduce-scatter.38.cloned.1.call-update) | async-done | bytes 272
  672.6 62.8 %reduce-scatter.40.cloned.1.call-done = bf16[64,2]{1,0:T(8,128)(2,1)} async-done(((bf16[512,2]{1,0:T(8,128)(2,1)}), bf16[64,2]{1,0:T(8,128)(2,1)}) %reduce-scatter.40.cloned.1.call-update) | async-done | bytes 272
  736.1 62.8 %reduce-scatter.44.cloned.1.call-done = bf16[64,2]{1,0:T(8,128)(2,1)} async-done(((bf16[512,2]{1,0:T(8,128)(2,1)}), bf16[64,2]{1,0:T(8,128)(2,1)}) %reduce-scatter.44.cloned.1.call-update) | async-done | bytes 272
  799.7 63.2 %reduce-scatter.34.cloned.1.call-done = bf16[64,8]{1,0:T(8,128)(2,1)} async-done(((bf16[512,8]{1,0:T(8,128)(2,1)}), bf16[64,8]{1,0:T(8,128)(2,1)}) %reduce-scatter.34.cloned.1.call-update) | async-done | bytes 1040
  863.6 64.4 %reduce-scatter.42.cloned.1.call-done = bf16[256,2]{1,0:T(8,128)(2,1)} async-done(((bf16[2048,2]{1,0:T(8,128)(2,1)}), bf16[256,2]{1,0:T(8,128)(2,1)}) %reduce-scatter.42.cloned.1.call-update) | async-done | bytes 1040
  929.0 5.8 all-reduce.3
  939.2 38.4 %all-reduce.7.cloned.1.call-done = (bf16[2,64,1536]{2,1,0:T(8,128)(2,1)}, bf16[2,64,512]{2,1,0:T(8,128)(2,1)}, bf16[2,64,2048]{2,1,0:T(8,128)(2,1)}, bf16[2,256,512]{2,1,0:T(8,128)(2,1)}, bf16[64,2048]{1,0:T(8,128)(2,1)}) async-done(((bf16[2,64,1536]{2,1,0:T(8,128)(2,1)}, bf16[2,64,512]{2,1,0:T(8,128)(2,1)}, bf16[2,64,2048]{2,1,0:T(8,128)(2,1)}, bf16[2,256,512]{2,1,0:T(8,128)(2,1)}, ...) | async-done | bytes 1835024 | tf_op jit(solution)/shard_map/psum | solution.py:205
  (358 shorter events, 138.6 us)
Async XLA Ops:
  7.2 7.1 copy-start.53
  7.2 7.1 copy-start.50
  7.2 7.1 copy-start.69
  7.3 206.6 %reduce-scatter.26.cloned.1.call-start = ((), (), s32[]{:S(2)}) async-start(), calls=%async_computation.12 | async-start | bytes 1179648 | tf_op jit(solution)/shard_map/reduce_scatter | solution.py:204
  13.7 36.2 %copy-start.55 = (f32[1,2048]{1,0:T(1,128)}, f32[1,2048]{1,0:T(1,128)S(1)}, u32[]{:S(2)}) copy-start(f32[1,2048]{1,0:T(1,128)S(1)} %get-tuple-element.128) | copy-start | bytes 24580
  22.5 25.3 %copy-start.1 = (f32[448,512]{1,0:T(8,128)}, f32[448,512]{1,0:T(8,128)S(1)}, u32[]{:S(2)}) copy-start(f32[448,512]{1,0:T(8,128)S(1)} %reshape.334) | copy-start | bytes 2752516
  49.9 12.0 %copy-start.72 = (f32[1,512]{1,0:T(1,128)S(1)}, f32[1,512]{1,0:T(1,128)}, u32[]{:S(2)}) copy-start(f32[1,512]{1,0:T(1,128)} %get-tuple-element.132) | copy-start | bytes 6148
  49.9 12.0 %copy-start.74 = (bf16[2,2048,512]{2,1,0:T(8,128)(2,1)S(1)}, bf16[2,2048,512]{2,1,0:T(8,128)(2,1)}, u32[]{:S(2)}) copy-start(bf16[2,2048,512]{2,1,0:T(8,128)(2,1)} %param.28) | copy-start | bytes 12582916
  89.9 10.5 %copy-start.10 = (bf16[448,512]{1,0:T(8,128)(2,1)S(1)}, bf16[448,512]{1,0:T(8,128)(2,1)}, u32[]{:S(2)}) copy-start(bf16[448,512]{1,0:T(8,128)(2,1)} %copy-done.9) | copy-start | bytes 1376260
  89.9 10.5 %copy-start.70 = (f32[1,512]{1,0:T(1,128)S(1)}, f32[1,512]{1,0:T(1,128)}, u32[]{:S(2)}) copy-start(f32[1,512]{1,0:T(1,128)} %get-tuple-element.131) | copy-start | bytes 6148
  89.9 10.5 %copy-start.75 = (bf16[2,2048,512]{2,1,0:T(8,128)(2,1)S(1)}, bf16[2,2048,512]{2,1,0:T(8,128)(2,1)}, u32[]{:S(2)}) copy-start(bf16[2,2048,512]{2,1,0:T(8,128)(2,1)} %param.28) | copy-start | bytes 12582916
  125.1 7.3 copy-start.8
  136.8 7.2 copy-start.18
  147.4 137.2 %reduce-scatter.32.cloned.1.call-start = ((), (), s32[]{:S(2)}) async-start(), calls=%async_computation.15 | async-start | bytes 2359296 | tf_op jit(solution)/shard_map/reduce_scatter | solution.py:204
  153.5 208.4 %reduce-scatter.24.cloned.1.call-start = ((), (), s32[]{:S(2)}) async-start(), calls=%async_computation.11 | async-start | bytes 3538944 | tf_op jit(solution)/shard_map/reduce_scatter | solution.py:204
  179.2 273.6 %reduce-scatter.28.cloned.1.call-start = ((), (), s32[]{:S(2)}) async-start(), calls=%async_computation.13 | async-start | bytes 4718592 | tf_op jit(solution)/shard_map/reduce_scatter | solution.py:204
  186.4 357.7 %reduce-scatter.30.cloned.1.call-start = ((), (), s32[]{:S(2)}) async-start(), calls=%async_computation.14 | async-start | bytes 4718592 | tf_op jit(solution)/shard_map/reduce_scatter | solution.py:204
  194.1 414.1 %reduce-scatter.36.cloned.1.call-start = ((), (), s32[]{:S(2)}) async-start(), calls=%async_computation.17 | async-start | bytes 147456
  195.2 9.1 copy-start.17
  199.8 471.9 %reduce-scatter.38.cloned.1.call-start = ((), (), s32[]{:S(2)}) async-start(), calls=%async_computation.18 | async-start | bytes 147456
  200.8 534.5 %reduce-scatter.40.cloned.1.call-start = ((), (), s32[]{:S(2)}) async-start(), calls=%async_computation.19 | async-start | bytes 147456
  201.7 597.1 %reduce-scatter.44.cloned.1.call-start = ((), (), s32[]{:S(2)}) async-start(), calls=%async_computation.21 | async-start | bytes 147456
  202.7 660.2 %reduce-scatter.34.cloned.1.call-start = ((), (), s32[]{:S(2)}) async-start(), calls=%async_computation.16 | async-start | bytes 147456
  205.6 338.5 %copy-start.67 = (bf16[2048]{0:T(1024)(128)(2,1)S(1)}, bf16[2048]{0:T(1024)(128)(2,1)}, u32[]{:S(2)}) copy-start(bf16[2048]{0:T(1024)(128)(2,1)} %param.32) | copy-start | bytes 12292
  206.9 338.3 %copy-start.13 = (bf16[64,2048]{1,0:T(8,128)(2,1)S(1)}, bf16[64,2048]{1,0:T(8,128)(2,1)}, u32[]{:S(2)}) copy-start(bf16[64,2048]{1,0:T(8,128)(2,1)} %param.33) | copy-start | bytes 786436
  206.9 340.3 %copy-start.62 = (bf16[512]{0:T(512)(128)(2,1)S(1)}, bf16[512]{0:T(512)(128)(2,1)}, u32[]{:S(2)}) copy-start(bf16[512]{0:T(512)(128)(2,1)} %get-tuple-element.75) | copy-start | bytes 3076
  206.9 360.9 %copy-start.29 = (f32[64,512]{1,0:T(8,128)S(1)}, f32[64,512]{1,0:T(8,128)}, u32[]{:S(2)}) copy-start(f32[64,512]{1,0:T(8,128)} %copy-done.28) | copy-start | bytes 393220
  207.9 336.2 %copy-start.25 = (bf16[448,512]{1,0:T(8,128)(2,1)S(1)}, bf16[448,512]{1,0:T(8,128)(2,1)}, u32[]{:S(2)}) copy-start(bf16[448,512]{1,0:T(8,128)(2,1)} %get-tuple-element.108) | copy-start | bytes 1376260
  207.9 337.4 %copy-start.80 = (u32[32]{0:T(128)S(1)}, u32[32]{0:T(128)}, u32[]{:S(2)}) copy-start(u32[32]{0:T(128)} %constant.107) | copy-start | bytes 388
  210.0 718.0 %reduce-scatter.42.cloned.1.call-start = ((), (), s32[]{:S(2)}) async-start(), calls=%async_computation.20 | async-start | bytes 589824
  211.9 765.7 %all-reduce.7.cloned.1.call-start = ((), (), s32[]{:S(2)}) async-start(), calls=%async_computation.22 | async-start | bytes 3670016 | tf_op jit(solution)/shard_map/psum | solution.py:205
  977.6 7.9 copy-start.40
  (68 other events, 225.2 us)
Sparse Core Ops, SparseCore 0:
  147.6 66.2 reduce-scatter.25
  217.8 66.7 reduce-scatter.31
  288.7 73.2 reduce-scatter.23
  365.9 86.9 reduce-scatter.27
  456.4 87.6 reduce-scatter.29
  547.6 60.5 reduce-scatter.35
  611.9 59.8 reduce-scatter.37
  675.4 59.8 reduce-scatter.39
  739.0 59.8 reduce-scatter.43
  803.0 59.8 reduce-scatter.33
  867.1 60.8 reduce-scatter.41
  930.6 46.9 all-reduce.6

commit v2 on v1

v2 whole, which is shorter than its diff:
```python
import functools

import jax
import jax.numpy as jnp
from jax import lax
from jax.experimental import pallas as pl
from jax.experimental.pallas import tpu as pltpu
from jax.sharding import PartitionSpec as P

HEADS = 8
EPS = 1e-05
MASKED = -1e30
F32 = jnp.float32
BF16 = jnp.bfloat16
MESH = pl.DeviceIdType.MESH
SHARDS = 8
PIECE = 16
GROUPS_OUT = 7
SLOTS = 3


def mm(left, right):
    return jnp.dot(left, right, preferred_element_type=F32)


def mm_right(left, right):
    return lax.dot_general(left, right, (((1,), (1,)), ((), ())), preferred_element_type=F32)


def flipped(value, mask):
    return value + mask - 2 * mask * ((value // mask) % 2)


def normalised(values):
    centre = values - jnp.mean(values, axis=-1, keepdims=True)
    scale = lax.rsqrt(jnp.mean(centre * centre, axis=-1, keepdims=True) + EPS)
    return centre * scale, scale


def gelu_both(v):
    size = jnp.abs(v)
    t = 1.0 / (1.0 + (0.3275911 * 0.7071067811865476) * size)
    bell = jnp.exp(-0.5 * (v * v))
    poly = t * (
        0.127414796
        + t * (-0.142248368 + t * (0.7107068705 + t * (-0.7265760135 + t * 0.5307027145)))
    )
    tail = poly * bell
    cdf = jnp.where(v >= 0, 1.0 - tail, tail)
    return v * cdf, cdf + v * (bell * 0.3989422804014327)


PARTS = {
    "a": (slice(0, 2), ("x", "y", "zl", "zh")),
    "b": (slice(2, 3), ("y", "x", "zl", "zh")),
    "c": (slice(3, 4), ("zl", "zh", "x", "y")),
}
AXES = ("y", "zh", "zl", "x")


def kernel(rem, plan, *refs):
    (
        pieces_ref, counts_ref, groups_ref, table_ref, again_ref, abias_ref, fgain_ref, ubias_ref, dbias_ref,
        egain_ref, pbias_ref, cot_ref, wqkv_hbm, wout_hbm, wup_hbm, wdown_hbm, wpool_hbm,
        emb_ref, dx_ref, fin_ref, small_ref,
        wqkv, wout, wup, wdown, wpool, es, ex, x3, x0, hs, nb, qkv, prob, ctx, act, dg, dyw, dyb, dqkv, wide, tmp, npool, upool,
        g_buf, r0, ra, rb, rc, f_buf, s_buf, w_sem, send_sem, recv_sem, sm_send, sm_recv, out_sem,
    ) = refs
    entries, slots, width = pieces_ref.shape
    layers = again_ref.shape[0]
    token_rows = slots * entries
    b = lax.axis_index("dp") // rem
    s = lax.axis_index("section")
    bits = {"zh": b // 4, "zl": (b // 2) % 2, "x": b % 2, "y": s // 2, "core": s % 2}
    dp_mask = {"zh": 4 * rem, "zl": 2 * rem, "x": rem, "y": 0, "core": 0}
    sec_mask = {"zh": 0, "zl": 0, "x": 0, "y": 2, "core": 1}

    def partner(axis):
        d, e = lax.axis_index("dp"), lax.axis_index("section")
        return (
            flipped(d, dp_mask[axis]) if dp_mask[axis] else d,
            flipped(e, sec_mask[axis]) if sec_mask[axis] else e,
        )

    barrier = pltpu.get_barrier_semaphore()
    for axis in bits:
        pl.semaphore_signal(barrier, inc=1, device_id=partner(axis), device_id_type=MESH)

    loads = {}
    order = []
    for layer in range(layers):
        order += [("qkv", layer, wqkv_hbm, wqkv), ("out", layer, wout_hbm, wout), ("up", layer, wup_hbm, wup), ("down", layer, wdown_hbm, wdown)]
    for at, (name, layer, source, target) in enumerate(order):
        loads[name, layer] = pltpu.make_async_copy(source.at[layer], target.at[layer], w_sem.at[at])
        loads[name, layer].start()
    loads["pool", 0] = pltpu.make_async_copy(wpool_hbm, wpool, w_sem.at[len(order)])
    loads["pool", 0].start()

    def rows(j):
        return pl.ds(pl.multiple_of(j * entries, entries), entries)

    def column(row_ref):
        eye = lax.broadcasted_iota(jnp.int32, (entries, entries), 0) == lax.broadcasted_iota(
            jnp.int32, (entries, entries), 1
        )
        row = row_ref[...].astype(F32)
        return jnp.sum(jnp.where(eye, row, 0.0), axis=1, keepdims=True)

    count = column(counts_ref)
    group = column(groups_ref)

    head_of = lax.broadcasted_iota(jnp.int32, (width, 128), 0) // (width // HEADS)
    lane_of = lax.broadcasted_iota(jnp.int32, (width, 128), 1) % 64
    head_of_t = lax.broadcasted_iota(jnp.int32, (128, width), 1) // (width // HEADS)
    lane_of_t = lax.broadcasted_iota(jnp.int32, (128, width), 0)
    scaling = (width // HEADS) ** -0.5
    for j in range(slots):
        es[j] = jnp.where(lane_of - head_of == j * HEADS, scaling, 0.0).astype(BF16)
        ex[j] = jnp.where(lane_of_t - head_of_t == j * HEADS, 1.0, 0.0).astype(BF16)
    live_lanes = (
        (lax.broadcasted_iota(jnp.int32, (entries, 128), 1) % 64) // HEADS
    ).astype(F32) < count

    x3[:, 0:slots, :] = pieces_ref[...].astype(F32)
    group_rows = jnp.zeros((entries, width), F32)
    for g in range(table_ref.shape[0]):
        group_rows = jnp.where(group == g, table_ref[g : g + 1, :].astype(F32), group_rows)
    for j in range(slots):
        x0[j * entries : (j + 1) * entries, :] = x3[:, j, :] + group_rows

    def norm_rows(source, gain):
        @pl.loop(0, slots)
        def _(j):
            n, _r = normalised(source[rows(j), :].astype(F32))
            nb[rows(j), :] = (n * gain).astype(BF16)

    def rolled(value, op):
        for shift in (8, 16, 32):
            value = op(value, pltpu.roll(value, shift, 1))
        return value

    def spread_rows(block, value):
        n = value.shape[-1]
        return (value.reshape(slots, entries, n) * block[None]).reshape(token_rows, n)

    def attention_forward(layer, source, target):
        norm_rows(source, again_ref[layer : layer + 1, :].astype(F32))
        loads["qkv", layer].wait()
        for t in range(3):
            cols = pl.ds(t * width, width)
            qkv[layer, :, cols] = mm(nb[...], wqkv[layer, :, cols]).astype(BF16)
        scores = jnp.zeros((token_rows, 128), F32)
        for j in range(slots):
            k = qkv[layer, rows(j), width : 2 * width]
            scores += mm(spread_rows(k, qkv[layer, :, 0:width]), es[j])
        scores = jnp.where(live_lanes[None], scores.reshape(slots, entries, 128), MASKED).reshape(token_rows, 128)
        raised = jnp.exp(scores - rolled(scores, jnp.maximum))
        p = raised / rolled(raised, jnp.add)
        prob[layer] = p
        p_low = p.astype(BF16)

        @pl.loop(0, width // 128)
        def _(c):
            lanes = pl.ds(pl.multiple_of(c * 128, 128), 128)
            v_lanes = pl.ds(pl.multiple_of(2 * width + c * 128, 128), 128)
            total = jnp.zeros((token_rows, 128), F32)
            for j in range(slots):
                total += spread_rows(qkv[layer, rows(j), v_lanes].astype(F32), mm(p_low, ex[j, :, lanes]))
            ctx[layer, :, lanes] = total.astype(BF16)

        loads["out", layer].wait()
        bias = abias_ref[layer : layer + 1, :].astype(F32)
        hs[target] = (source[...].astype(F32) + mm(ctx[layer], wout[layer]) + bias).astype(BF16)

    def ffn_forward(layer, source, target):
        norm_rows(source, fgain_ref[layer : layer + 1, :].astype(F32))
        loads["up", layer].wait()

        @pl.loop(0, wup.shape[2] // 256)
        def _(t):
            cols = pl.ds(pl.multiple_of(t * 256, 256), 256)
            inner = mm(nb[...], wup[layer, :, cols]) + ubias_ref[layer : layer + 1, cols].astype(F32)
            activated, slope = gelu_both(inner)
            act[layer, :, cols] = activated.astype(BF16)
            dg[layer, :, cols] = slope.astype(BF16)

        loads["down", layer].wait()
        bias = dbias_ref[layer : layer + 1, :].astype(F32)
        hs[target] = (source[...].astype(F32) + mm(act[layer], wdown[layer]) + bias).astype(BF16)

    def put_columns(slot, quantum, value):
        block = value.astype(BF16)
        for o in range(SHARDS):
            for y in range(2):
                for c in range(2):
                    at = o * 64 + y * 32 + c * PIECE
                    g_buf[slot, quantum, c, y, o // 4, (o // 2) % 2, o % 2] = block[at : at + PIECE]

    def put_down(slot, t, value):
        block = value.astype(BF16)
        for half in range(2):
            for k in range(4):
                for y in range(2):
                    for c in range(2):
                        at = half * 256 + k * 64 + y * 32 + c * PIECE
                        g_buf[slot, k, c, y, t // 2, t % 2, half] = block[at : at + PIECE]

    def col_sum(value):
        return jnp.sum(value, axis=0, keepdims=True)

    def own(view, lead, axis_list, axis, index, full=None):
        spots = [slice(None)] * lead + [index if a == axis else slice(None) for a in axis_list]
        return view.at[tuple(spots)]

    part_buffers = {"a": ra, "b": rb, "c": rc}

    def stage_views(g, part, stage):
        quanta, dims = PARTS[part]
        count_q = quanta.stop - quanta.start
        if stage == 0:
            slot = g % SLOTS
            core = bits["core"]
            source = g_buf.at[slot, quanta, 1 - core]
            mine = g_buf.at[slot, quanta, core]
            return "core", source, mine, r0.at[g, quanta]
        if stage <= 4:
            axis = dims[stage - 1]
            left = [a for a in AXES if a not in dims[: stage - 1]]
            before = r0.at[g, quanta] if stage == 1 else part_buffers[part][stage - 2].at[g]
            after = part_buffers[part][stage - 1].at[g]
            spots = [slice(None)] + [slice(None)] * len(left)
            spots[1 + left.index(axis)] = 1 - bits[axis]
            source = before.at[tuple(spots)]
            spots[1 + left.index(axis)] = bits[axis]
            return axis, source, before.at[tuple(spots)], after
        y, core = bits["y"], bits["core"]
        if stage == 5:
            view = f_buf.at[g, quanta, y, core]
            return "y", view, None, view
        view = f_buf.at[g, quanta, :, core]
        return "core", view, None, view

    part_at = {"a": 0, "b": 1, "c": 2}

    def copy_of(g, part, stage):
        axis, source, mine, landing = stage_views(g, part, stage)
        at = part_at[part]
        return pltpu.make_async_remote_copy(
            src_ref=source,
            dst_ref=landing,
            send_sem=send_sem.at[g, at, stage],
            recv_sem=recv_sem.at[g, at, stage],
            device_id=partner(axis),
            device_id_type=MESH,
        )

    def start(g, part, stage):
        copy_of(g, part, stage).start()

    def finish(g, part, stage):
        axis, source, mine, landing = stage_views(g, part, stage)
        copy_of(g, part, stage).wait()
        if stage < 4:
            landing[...] = landing[...] + mine[...]
        elif stage == 4:
            quanta = PARTS[part][0]
            f_buf[g, quanta, bits["y"], bits["core"]] = landing[...] + mine[...]

    def advance(g, part, stage):
        if stage >= 0:
            finish(g, part, stage)
        if stage < 6:
            start(g, part, stage + 1)

    def small_copy(stage):
        axis = ("core", "x", "y", "zl", "zh")[stage]
        return pltpu.make_async_remote_copy(
            src_ref=s_buf.at[2 * stage],
            dst_ref=s_buf.at[2 * stage + 1],
            send_sem=sm_send.at[stage],
            recv_sem=sm_recv.at[stage],
            device_id=partner(axis),
            device_id_type=MESH,
        )

    def small(stage):
        if stage >= 0:
            small_copy(stage).wait()
            s_buf[2 * stage + 2] = s_buf[2 * stage] + s_buf[2 * stage + 1]
        if stage < 4:
            small_copy(stage + 1).start()

    def put_small(at, value):
        s_buf[0, pl.ds(at, value.shape[0]), :] = value

    def forward():
        for layer in range(layers):
            attention_forward(layer, x0 if layer == 0 else hs.at[2 * layer - 1], 2 * layer)
            ffn_forward(layer, hs.at[2 * layer], 2 * layer + 1)

        live_sum = jnp.zeros((entries, width), F32)
        for j in range(slots):
            n, _r = normalised(hs[2 * layers - 1, rows(j), :].astype(F32))
            live_sum += jnp.where(count > j, n, 0.0)
        npool[...] = live_sum / count
        pooled = (npool[...] * egain_ref[...].astype(F32)).astype(BF16)
        pooled_t = pooled.astype(F32).T.astype(BF16)
        loads["pool", 0].wait()
        for k in range(4):
            put_columns(0, k, mm(pooled_t, cot_ref[:, k * width : (k + 1) * width]))

    def embed():
        pooled = (npool[...] * egain_ref[...].astype(F32)).astype(BF16)
        for k in range(4):
            cols = slice(k * width, (k + 1) * width)
            emb_ref[:, cols] = (mm(pooled, wpool[:, cols]) + pbias_ref[:, cols].astype(F32)).astype(BF16)

    def pool_backward():
        for k in range(4):
            put_small(17 + k, col_sum(cot_ref[:, k * width : (k + 1) * width].astype(F32)))
        d_pooled = mm_right(cot_ref[...], wpool[...]).astype(BF16).astype(F32)
        put_small(16, col_sum(d_pooled * npool[...]))
        upool[...] = d_pooled * egain_ref[...].astype(F32) / count
        for j in range(slots):
            n, r = normalised(hs[2 * layers - 1, rows(j), :].astype(F32))
            u = jnp.where(count > j, upool[...], 0.0)
            d = r * (u - jnp.mean(u, axis=-1, keepdims=True) - n * jnp.mean(u * n, axis=-1, keepdims=True))
            dyb[rows(j), :] = d.astype(BF16)

    def norm_backward(source, gain, at, keep_wide):
        def step(j, total):
            n, r = normalised(source[rows(j), :].astype(F32))
            d_normed = wide[rows(j), :]
            u = d_normed * gain
            d = r * (u - jnp.mean(u, axis=-1, keepdims=True) - n * jnp.mean(u * n, axis=-1, keepdims=True))
            d_h = dyb[rows(j), :].astype(F32) + d
            dyb[rows(j), :] = d_h.astype(BF16)
            if keep_wide:
                wide[rows(j), :] = d_h
            return total + d_normed * n

        total = lax.fori_loop(0, slots, step, jnp.zeros((entries, width), F32))
        put_small(at, col_sum(total))

    def dy_sum(at):
        put_small(at, col_sum(dyb[...].astype(F32)))

    def turned(value):
        return value.astype(F32).T.astype(BF16)

    def down_grad(layer, slot):
        dy_sum(8 * layer + 3)

        @pl.loop(0, 4)
        def _(t):
            cols = pl.ds(pl.multiple_of(t * width, width), width)
            put_down(slot, t, mm(turned(act[layer, :, cols]), dyb[...]))

    def up_grad(layer, slot, source):
        gain = fgain_ref[layer : layer + 1, :].astype(F32)
        norm_rows(source, gain)
        tmp[...] = turned(nb[...])

        @pl.loop(0, 4)
        def _(t):
            cols = pl.ds(pl.multiple_of(t * width, width), width)
            d_act = mm_right(dyb[...], wdown[layer, cols, :])
            d_inner = (d_act * dg[layer, :, cols].astype(F32)).astype(BF16)
            put_small(8 * layer + 4 + t, col_sum(d_inner.astype(F32)))
            put_columns(slot, t, mm(tmp[...], d_inner))
            dqkv[:, cols] = d_inner

        wide[...] = mm_right(dqkv[...], wup[layer])
        norm_backward(source, gain, 8 * layer + 2, False)

    def attention_grad(layer, slot, source):
        gain = again_ref[layer : layer + 1, :].astype(F32)
        dy_sum(8 * layer + 1)
        put_columns(slot, 3, mm(turned(ctx[layer]), dyb[...]))
        nb[...] = mm_right(dyb[...], wout[layer]).astype(BF16)
        d_prob = jnp.zeros((token_rows, 128), F32)
        for j in range(slots):
            v = qkv[layer, rows(j), 2 * width : 3 * width]
            d_prob += mm(spread_rows(v, nb[...]), es[j])
        d_prob = d_prob * (1.0 / scaling)
        p = prob[layer]
        p_low = p.astype(BF16)
        mixed = p * d_prob
        d_scores = (mixed - p * rolled(mixed, jnp.add)).astype(BF16)

        @pl.loop(0, width // 128)
        def _(c):
            def lanes(part):
                return pl.ds(pl.multiple_of(part * width + c * 128, 128), 128)

            d_q = jnp.zeros((token_rows, 128), F32)
            for j in range(slots):
                weights = mm(p_low, ex[j, :, lanes(0)])
                d_v = jnp.sum((weights * nb[:, lanes(0)].astype(F32)).reshape(slots, entries, 128), axis=0)
                weights = mm(d_scores, ex[j, :, lanes(0)])
                d_q += spread_rows(qkv[layer, rows(j), lanes(1)].astype(F32), weights)
                d_k = jnp.sum((weights * qkv[layer, :, lanes(0)].astype(F32)).reshape(slots, entries, 128), axis=0)
                dqkv[rows(j), lanes(1)] = (d_k * scaling).astype(BF16)
                dqkv[rows(j), lanes(2)] = d_v.astype(BF16)
            dqkv[:, lanes(0)] = (d_q * scaling).astype(BF16)

        norm_rows(source, gain)
        tmp[...] = turned(nb[...])
        for t in range(3):
            put_columns(slot, t, mm(tmp[...], dqkv[:, t * width : (t + 1) * width]))
        wide[...] = mm_right(dqkv[:, 0 : 3 * width], wqkv[layer])
        norm_backward(source, gain, 8 * layer, layer == 0)

    def finish_input():
        sums = jnp.zeros((entries, width), F32)
        for j in range(slots):
            sums += wide[j * entries : (j + 1) * entries, :]
            x3[:, j, :] = wide[j * entries : (j + 1) * entries, :]
        dx_ref[...] = x3[:, 0:slots, :].astype(BF16)
        for g in range(table_ref.shape[0]):
            put_small(24 + g, col_sum(jnp.where(group == g, sums, 0.0)))

    s_buf[0] = jnp.zeros(s_buf.shape[1:], F32)

    computations = {
        "forward": forward,
        "embed": embed,
        "pool_backward": pool_backward,
        "down1": lambda: down_grad(1, 1 % SLOTS),
        "up1": lambda: up_grad(1, 2 % SLOTS, hs.at[2]),
        "attn1": lambda: attention_grad(1, 3 % SLOTS, hs.at[1]),
        "down0": lambda: down_grad(0, 4 % SLOTS),
        "up0": lambda: up_grad(0, 5 % SLOTS, hs.at[0]),
        "attn0": lambda: attention_grad(0, 6 % SLOTS, x0),
        "input": finish_input,
    }
    entered = False
    for item in plan:
        if item[0] == "compute":
            computations[item[1]]()
            continue
        if not entered:
            pl.semaphore_wait(barrier, 5)
            entered = True
        if item[0] == "advance":
            advance(*item[1:])
        elif item[0] == "small":
            small(item[1])
    done = pltpu.make_async_copy(f_buf, fin_ref, out_sem)
    done.start()
    small_ref[...] = s_buf[10]
    done.wait()


def plan_of():
    names = ["forward", "down1", "up1", "attn1", "down0", "up0", "attn0"]
    plan = []
    for tick in range(GROUPS_OUT + 7):
        if tick < GROUPS_OUT:
            plan.append(("compute", names[tick]))
            for part in PARTS:
                plan.append(("advance", tick, part, -1))
        if tick == 0:
            plan.append(("compute", "pool_backward"))
        if tick == 1:
            plan.append(("compute", "embed"))
        if tick == 6:
            plan.append(("compute", "input"))
            plan.append(("small", -1))
        if tick > 6 and tick < 12:
            plan.append(("small", tick - 7))
        for g in range(GROUPS_OUT):
            stage = tick - 1 - g
            if 0 <= stage <= 6:
                for part in PARTS:
                    plan.append(("advance", g, part, stage))
    return tuple(plan)


def per_device(rem, plan, pieces, counts, groups, table, again, wqkv, wout, abias, fgain, wup, ubias, wdown, dbias, egain, wpool, pbias, cot):
    entries, slots, width = pieces.shape
    hidden = wup.shape[2]
    layers = wqkv.shape[0]
    token_rows = entries * slots
    vmem = pl.BlockSpec(memory_space=pltpu.VMEM)
    hbm = pl.BlockSpec(memory_space=pl.ANY)
    tile = (PIECE, width)

    def buffers(part):
        quanta, dims = PARTS[part]
        size = quanta.stop - quanta.start
        return [pltpu.VMEM((GROUPS_OUT, size) + (2,) * (3 - k) + tile, BF16) for k in range(4)]

    def body(*refs):
        refs = list(refs)
        fixed = 17 + 4 + 25
        head, rest = refs[: fixed], refs[fixed:]
        parts = [rest[4 * k : 4 * k + 4] for k in range(3)]
        kernel(rem, plan, *head, *parts, *rest[12:])

    scratch = [
        pltpu.VMEM(wqkv.shape, BF16), pltpu.VMEM(wout.shape, BF16), pltpu.VMEM(wup.shape, BF16), pltpu.VMEM(wdown.shape, BF16),
        pltpu.VMEM(wpool.shape, BF16), pltpu.VMEM((slots, width, 128), BF16), pltpu.VMEM((slots, 128, width), BF16),
        pltpu.VMEM((entries, 8, width), F32), pltpu.VMEM((token_rows, width), F32), pltpu.VMEM((2 * layers, token_rows, width), BF16),
        pltpu.VMEM((token_rows, width), BF16), pltpu.VMEM((layers, token_rows, 3 * width), BF16), pltpu.VMEM((layers, token_rows, 128), F32),
        pltpu.VMEM((layers, token_rows, width), BF16), pltpu.VMEM((layers, token_rows, hidden), BF16), pltpu.VMEM((layers, token_rows, hidden), BF16),
        pltpu.VMEM((8, 128), F32), pltpu.VMEM((token_rows, width), BF16), pltpu.VMEM((token_rows, hidden), BF16), pltpu.VMEM((token_rows, width), F32),
        pltpu.VMEM((width, token_rows), BF16), pltpu.VMEM((entries, width), F32), pltpu.VMEM((entries, width), F32),
        pltpu.VMEM((SLOTS, 4, 2, 2, 2, 2, 2) + tile, BF16), pltpu.VMEM((GROUPS_OUT, 4, 2, 2, 2, 2) + tile, BF16),
        *buffers("a"), *buffers("b"), *buffers("c"),
        pltpu.VMEM((GROUPS_OUT, 4, 2, 2) + tile, BF16), pltpu.VMEM((11, 32, width), F32),
        pltpu.SemaphoreType.DMA((4 * layers + 1,)), pltpu.SemaphoreType.DMA((GROUPS_OUT, 3, 7)), pltpu.SemaphoreType.DMA((GROUPS_OUT, 3, 7)),
        pltpu.SemaphoreType.DMA((5,)), pltpu.SemaphoreType.DMA((5,)), pltpu.SemaphoreType.DMA,
    ]
    emb, dx, fin, small = pl.pallas_call(
        body,
        out_shape=(
            jax.ShapeDtypeStruct((entries, wpool.shape[1]), BF16),
            jax.ShapeDtypeStruct(pieces.shape, BF16),
            jax.ShapeDtypeStruct((GROUPS_OUT, 4, 2, 2) + tile, BF16),
            jax.ShapeDtypeStruct((32, width), F32),
        ),
        in_specs=[vmem] * 12 + [hbm] * 5,
        out_specs=(vmem, vmem, hbm, vmem),
        scratch_shapes=scratch,
        compiler_params=pltpu.CompilerParams(collective_id=0, has_side_effects=True, vmem_limit_bytes=64 * 2**20),
    )(
        pieces, counts.reshape(1, -1), groups.reshape(1, -1), table, again, abias, fgain, ubias, dbias,
        egain.reshape(1, -1), pbias.reshape(1, -1), cot, wqkv, wout, wup, wdown, wpool,
    )
    return emb, dx, fin, small


def unpack(rem, emb, dx, fin, small):
    wide = fin.reshape(GROUPS_OUT, 4, 64, fin.shape[-1]).astype(F32)

    def columns(group, lo, hi):
        return jnp.concatenate([wide[group, k] for k in range(lo, hi)], axis=-1)

    down = jnp.stack([wide[4].reshape(256, -1), wide[1].reshape(256, -1)])
    up = jnp.stack([columns(5, 0, 4), columns(2, 0, 4)])
    out = jnp.stack([wide[6, 3], wide[3, 3]])
    qkv = jnp.stack([columns(6, 0, 3), columns(3, 0, 3)])
    pool = columns(0, 0, 4)
    part = lax.axis_index("dp") // rem

    def share(value):
        return lax.dynamic_slice_in_dim(value, part * (value.shape[-1] // SHARDS), value.shape[-1] // SHARDS, value.ndim - 1)

    layered = [share(jnp.stack([small[k], small[8 + k]])) for k in range(4)]
    ubias = share(jnp.stack([small[4:8].reshape(-1), small[12:16].reshape(-1)]))
    grads = [
        (share(small[24:32]), 1), (layered[0], 1), (qkv, 1), (out, 1), (layered[1], 1), (layered[2], 1), (up, 1), (ubias, 1),
        (down, 1), (layered[3], 1), (share(small[16]), 0), (pool, 0), (share(small[17:21].reshape(-1)), 0),
    ]
    if rem > 1:
        blocks = [list(range(k * rem, (k + 1) * rem)) for k in range(SHARDS)]
        grads = [
            (lax.psum_scatter(g, "dp", scatter_dimension=d, axis_index_groups=blocks, tiled=True), d) for g, d in grads
        ]
    return (emb, dx, *[g for g, d in grads])


def solution(mesh):
    rem = mesh.shape["dp"] // SHARDS
    plan = plan_of()

    def whole(*args):
        return unpack(rem, *per_device(rem, plan, *args))

    placed = (P(("dp", "section"), None, None), P(("dp", "section")), P(("dp", "section"))) + (P(),) * 13 + (P(("dp", "section"), None),)
    return jax.shard_map(
        whole,
        mesh=mesh,
        in_specs=placed,
        out_specs=(
            P(("dp", "section"), None), P(("dp", "section"), None, None), P(None, "dp"), P(None, "dp"), P(None, "dp", None), P(None, "dp", None),
            P(None, "dp"), P(None, "dp"), P(None, "dp", None), P(None, "dp"), P(None, "dp", None), P(None, "dp"), P("dp"), P("dp", None), P("dp"),
        ),
        check_vma=False,
    )
```

time: 1000 us -> 149 us (0.15)
  waiting for transfers between devices: 726 us -> 0 us
  Pallas kernels: 0 us -> 127 us
  matrix products: 102 us -> 0 us
  local copies, waits for them, and re-layouts: 71.1 us -> 13.2 us
  other arithmetic: 51 us -> 7.16 us
  blocking collectives: 26.2 us -> 0 us
  between operations: 17 us -> 0.74 us
    unnamed x18 -> x0, waiting for transfers between devices: 355 us -> none
    reduce_scatter x5 -> x0, waiting for transfers between devices: 332 us -> none  [reduced(): lax.psum_scatter(term.astype(jnp.bfloat16), 'dp', scatter_dimension=dim,...]
    pallas_call x0 -> x1, Pallas kernels: none -> 127 us  [per_device(): pl.pallas_call(body, out_shape=(jax.ShapeDtypeStruct((entries, wpool.shap...]
    dot_general x39 -> x0, matrix products: 92.1 us -> none  [the longest x10 35.6 us: matmul_plain(): return jnp.dot(left_side, right_side, preferred_element_type=jnp.float32)]
    psum x1 -> x0, waiting for transfers between devices: 38.4 us -> none  [reduced(): return wide(lax.psum(part, 'section'))]
    reshape x14 -> x2, local copies, waits for them, and re-layouts: 24.4 us -> 2.55 us  [the longest x1 1.29 us: per_device(): pbias.reshape(1, -1)]
    convert_element_type x21 -> x1, other arithmetic: 21.4 us -> 0.51 us  [unpack(): wide = fin.reshape(GROUPS_OUT, 4, 64, fin.shape[-1]).astype(F32)]
    unnamed x1 -> x0, blocking collectives: 20.4 us -> none
  transfers between devices with their start and end apart: 12 -> 0, of which waited for: 12 -> 0; matrix products, arithmetic and copies ran while one was open for 7% -> 0% of each run, Pallas kernels for 0% -> 0%
where the time goes in v2:
time: 149 us; the launch traced here: 148 us
  Pallas kernels  127 us (85%)
  local copies, waits for them, and re-layouts  13.2 us (9%)
  other arithmetic  7.16 us (5%)
    pallas_call x1, Pallas kernels, per_device(): pl.pallas_call(body, out_shape=(jax.ShapeDtypeStruct((entries, wpool.shap...  127 us
    unnamed x11, local copies, waits for them, and re-layouts  5.52 us

profile of v2, /device:TPU:0, one launch (start us, length us, event | category | flops | bytes accessed | tf_op | source)
XLA Modules:
  0.0 148.1 jit_solution(3408509887406281681)
XLA Ops:
  0.7 1.3 reshape.54.refs_9_
  1.9 1.3 reshape.55.refs_10_
  3.2 2.1 %copy.32.refs_0_ = bf16[64,7,512]{2,1,0:T(8,128)(2,1)} copy(bf16[64,7,512]{2,0,1:T(8,128)(2,1)} %param.17) | data formatting | bytes 917504 | tf_op args[0]
  5.3 127.0 %shard_map.280 = (bf16[64,2048]{1,0:T(8,128)(2,1)}, bf16[64,7,512]{2,1,0:T(8,128)(2,1)}, bf16[7,4,2,2,16,512]{5,4,3,2,1,0:T(8,128)(2,1)}, f32[32,512]{1,0:T(8,128)}) custom-call(bf16[64,7,512]{2,1,0:T(8,128)(2,1)} %copy.32.refs_0_, s32[1,64]{1,0:T(1,128)} %bitcast.73, s32[1,64]{1,0:T(1,128)} %bitcast.74, bf16[8,512]{1,0:T(8,128)(2,1)} %refs_3_.1, ...), custom_call_target="tpu_custom_call" | custom-call | tf_op jit(solution)/shard_map/pallas_call | solution.py:515
  132.2 0.0 copy-start
  132.2 0.9 slice.107
  133.1 0.7 constant_dynamic-slice_fusion.1
  133.8 0.9 fusion.7
  134.7 0.8 slice_bitcast_fusion.20
  135.5 0.6 dynamic_slice.34
  136.1 0.6 fusion.5
  136.7 0.6 fusion.1
  137.3 0.6 fusion.3
  138.0 0.7 fusion
  138.7 2.0 %copy.33 = bf16[64,7,512]{2,0,1:T(8,128)(2,1)} copy(bf16[64,7,512]{2,1,0:T(8,128)(2,1)} %get-tuple-element.24) | data formatting | bytes 917504
  140.6 1.2 fusion.6
  141.8 1.0 pad_maximum_fusion.1
  142.8 0.0 copy-done
  142.8 0.5 convert_element_type.6
  143.4 0.3 slice_bitcast_fusion.3
  143.7 0.8 pad_maximum_fusion.3
  144.5 0.7 pad_maximum_fusion.4
  145.3 0.0 copy-start.1
  145.3 0.1 maximum_bitcast_fusion.2
  145.3 0.9 pad_maximum_fusion.2
  146.3 0.1 maximum_bitcast_fusion
  146.3 1.1 pad_maximum_fusion
  147.4 0.0 copy-done.1
  147.4 0.7 copy.38
  (4 shorter events, 0.0 us)
Async XLA Ops:
  132.2 10.6 %copy-start = (bf16[7,4,2,2,16,512]{5,4,3,2,1,0:T(8,128)(2,1)S(1)}, bf16[7,4,2,2,16,512]{5,4,3,2,1,0:T(8,128)(2,1)}, u32[]{:S(2)}) copy-start(bf16[7,4,2,2,16,512]{5,4,3,2,1,0:T(8,128)(2,1)} %get-tuple-element.22) | copy-start | bytes 5505028
  145.3 2.1 %copy-start.1 = (bf16[64,2048]{1,0:T(8,128)(2,1)S(1)}, bf16[64,2048]{1,0:T(8,128)(2,1)}, u32[]{:S(2)}) copy-start(bf16[64,2048]{1,0:T(8,128)(2,1)} %get-tuple-element.94) | copy-start | bytes 786436
